TPU v7x, 512 devices: a whole 4x8x8 slice. The times are simulated.
512 devices in a mesh: chan: 64 (over z, x, y_hi), rblk: 8 (over y_lo, core).
Axes of the slice: x: 4, y: 8 (y_hi: 2, y_lo: 4; y = y_hi * 4 + y_lo), z: 8, core: 2. Of those that a mesh axis runs over, the one named last changes fastest.
Arguments:
- records: bfloat16 [8, 5120, 7680], P(None, ('rblk', 'chan')), may hold values from -64 to 64
- source_index: int32 [64], replicated, may hold values from 0 to 5119, as said below
- band_edges: int32 [33], replicated, may hold values from 0 to 1536, as said below
Outputs:
- correlations: bfloat16 [1536, 2, 64, 5120], P('chan', None, None, 'rblk')
Inputs may be any that keep to these rules, and one draw needn't show every extreme that they name: `source_index`: 64 distinct channel numbers. `band_edges`: begins with 0, ends with 1536, and rises by 32 or more at every step.
All inputs are finite; a program needn't handle non-finite values.
Results may differ from a plain program's by a relative error of at most 0.001.
Values sent between devices are 32-bit elements; how exact they have to be, the bound alone decides.
No kernel may reach another device: no remote copies, remote signals or barrier semaphores. Data moves between devices by JAX's collectives and lax.ppermute only.
A program may use at most 128 MiB of HBM per device.

v0:
```python
import math

import jax
import jax.numpy as jnp
from jax import lax
from jax.sharding import PartitionSpec as P

TP = 60
TQ = 128
F_LOW = 7
NF = 1536


epsilon = 1e-06
clip_factor = 2.0
peak_value = lax.Precision.HIGHEST


def angle_table(rows_count, cols_count, modulus):
    row_index = jnp.arange(rows_count, dtype=jnp.int32)
    col_index = jnp.arange(cols_count, dtype=jnp.int32)
    product = row_index[:, None] * col_index[None, :] % modulus
    angles = product.astype(jnp.float32) * (2.0 * math.pi / modulus)
    return (jnp.cos(angles), jnp.sin(angles))


def forward_bins(clipped):
    row_count = clipped.shape[0]
    grid = clipped.reshape(row_count, TP, TQ)
    cos_first, sin_first = angle_table(TP, TP, TP)
    first_re = jnp.einsum("kn,cnm->ckm", cos_first, grid, precision=peak_value)
    first_im = -jnp.einsum("kn,cnm->ckm", sin_first, grid, precision=peak_value)
    cos_twist, sin_twist = angle_table(TP, TQ, TP * TQ)
    twist_re = first_re * cos_twist + first_im * sin_twist
    twist_im = first_im * cos_twist - first_re * sin_twist
    top_rows = (F_LOW + NF - 1) // TP + 1
    cos_second, sin_second = angle_table(top_rows, TQ, TQ)
    final_re = jnp.einsum("jm,ckm->cjk", cos_second, twist_re, precision=peak_value) + jnp.einsum(
        "jm,ckm->cjk", sin_second, twist_im, precision=peak_value
    )
    final_im = jnp.einsum("jm,ckm->cjk", cos_second, twist_im, precision=peak_value) - jnp.einsum(
        "jm,ckm->cjk", sin_second, twist_re, precision=peak_value
    )
    flat_re = final_re.reshape(row_count, top_rows * TP)[:, F_LOW : F_LOW + NF]
    flat_im = final_im.reshape(row_count, top_rows * TP)[:, F_LOW : F_LOW + NF]
    return (flat_re, flat_im)


def whiten(spec_re, spec_im, band_edges):
    bin_index = jnp.arange(spec_re.shape[-1], dtype=jnp.int32)
    member = (
        (bin_index[None, :] >= band_edges[:-1, None]) & (bin_index[None, :] < band_edges[1:, None])
    ).astype(jnp.float32)
    power = spec_re * spec_re + spec_im * spec_im
    band_total = jnp.dot(power, member.T, precision=peak_value)
    band_mean = band_total / jnp.sum(member, axis=1)
    per_bin = jnp.dot(band_mean, member, precision=peak_value)
    scaling = lax.rsqrt(per_bin + epsilon)
    return (spec_re * scaling, spec_im * scaling)


def spectra_block(records_part, band_edges):
    signal = records_part.astype(jnp.float32)
    amplitude = jnp.sqrt(jnp.mean(signal * signal, axis=-1, keepdims=True) + epsilon)
    clipped = jnp.clip(signal, -clip_factor * amplitude, clip_factor * amplitude)
    seg_count, chan_count, length = signal.shape
    spec_re, spec_im = forward_bins(clipped.reshape(seg_count * chan_count, length))
    white_re, white_im = whiten(spec_re, spec_im, band_edges)
    return jnp.stack(
        [white_re.reshape(seg_count, chan_count, NF), white_im.reshape(seg_count, chan_count, NF)]
    )


def pick_sources(source_index, spectra, first_channel):
    channel_ids = first_channel + jnp.arange(spectra.shape[2], dtype=jnp.int32)
    chooser = (source_index[:, None] == channel_ids[None, :]).astype(jnp.float32)
    return jnp.einsum("sr,gtrf->gtsf", chooser, spectra, precision=peak_value)


def shards(records, source_index, band_edges):
    local_part = spectra_block(records, band_edges)
    band_limited = lax.all_to_all(local_part, "chan", split_axis=3, concat_axis=2, tiled=True)
    receivers = band_limited.shape[2]
    first_channel = lax.axis_index("rblk") * receivers
    picked = pick_sources(source_index, band_limited, first_channel)
    source_list = lax.psum(picked, "rblk")
    transposed_rows = jnp.stack([band_limited[1], -band_limited[0]])
    real_component = jnp.einsum("ikev,ikwv->vew", source_list, band_limited, precision=peak_value)
    imaginary_component = jnp.einsum(
        "ikev,ikwv->vew", source_list, transposed_rows, precision=peak_value
    )
    stacked = jnp.stack([real_component, imaginary_component], axis=1) / band_limited.shape[1]
    return stacked.astype(jnp.bfloat16)


def solution(mesh):
    return jax.shard_map(
        shards,
        mesh=mesh,
        in_specs=(P(None, ("rblk", "chan"), None), P(), P()),
        out_specs=P("chan", None, None, "rblk"),
        check_vma=False,
    )
```

profile of v0, /device:TPU:1, one launch (start us, length us, event | category | flops | bytes accessed | tf_op | source)
XLA Modules:
  0.0 269.4 jit_solution(11322422250672623359)
XLA Ops:
  6.5 1.6 fusion.5
  8.2 1.7 fusion.6
  9.8 3.4 %copy.69 = f32[8,10,7680]{2,1,0:T(8,128)} copy(f32[8,10,7680]{2,0,1:T(8,128)S(1)} %fusion.6) | data formatting | bytes 4915200 | tf_op jit(solution)/shard_map/jit(clip)/min | solution.py:65
  13.2 4.7 %reshape_reshape.3 = f32[80,60,128]{2,1,0:T(8,128)} reshape(f32[8,10,7680]{2,1,0:T(8,128)} %copy.69) | data formatting | bytes 4915200 | tf_op jit(solution)/shard_map/reshape;reshape | solution.py:29
  18.0 4.4 %fusion.46 = f32[80,128,60]{1,2,0:T(8,128)S(1)} fusion(f32[80,60,128]{2,1,0:T(8,128)} %reshape_reshape.3), kind=kOutput, calls=%fused_computation.60 | convolution fusion | flops 442400384 | bytes 4915200 | tf_op jit(solution)/shard_map/kn,cnm->ckm/dot_general | solution.py:31
  22.4 2.6 fusion.44
  25.1 7.3 %fusion.20 = f32[80,60,26]{1,2,0:T(8,128)S(1)} fusion(f32[80,128,60]{1,2,0:T(8,128)S(1)} %fusion.46, f32[80,128,60]{1,2,0:T(8,128)S(1)} %fusion.44, f32[60,128]{1,0:T(8,128)S(1)} %get-tuple-element.13, f32[60,128]{1,0:T(8,128)S(1)} %get-tuple-element.14), kind=kOutput, calls=%fused_computation.30 | convolution fusion | flops 194196992 | bytes 5475840 | tf_op jit(solution)/shard_map/jm,ckm->cjk/dot_general | solution.py:38
  32.4 8.7 %fusion.16 = f32[80,60,26]{1,2,0:T(8,128)} fusion(f32[80,128,60]{1,2,0:T(8,128)S(1)} %fusion.46, f32[80,128,60]{1,2,0:T(8,128)S(1)} %fusion.44, f32[60,128]{1,0:T(8,128)S(1)} %get-tuple-element.13, f32[60,128]{1,0:T(8,128)S(1)} %get-tuple-element.14), kind=kOutput, calls=%fused_computation.29 | convolution fusion | flops 194196992 | bytes 5475840 | tf_op jit(solution)/shard_map/jm,ckm->cjk/dot_general | solution.py:41
  41.1 8.4 %fusion.9 = f32[80,26,60]{2,1,0:T(8,128)} fusion(f32[80,60,26]{1,2,0:T(8,128)S(1)} %fusion.20, f32[80,128,60]{1,2,0:T(8,128)S(1)} %fusion.46, f32[80,128,60]{1,2,0:T(8,128)S(1)} %fusion.44, f32[60,128]{1,0:T(8,128)S(1)} %get-tuple-element.13, f32[60,128]{1,0:T(8,128)S(1)} %get-tuple-element.14), kind=kOutput, calls=%fused_computation.22 | convolution fusion | flops 194321792 | bytes 5975040 | tf_op jit(solution)/shard_map/jm,ckm->cjk/dot_general | solution.py:38
  49.5 2.0 reshape.82
  51.5 10.5 %fusion.8 = f32[80,26,60]{2,1,0:T(8,128)} fusion(f32[80,60,26]{1,2,0:T(8,128)} %fusion.16, f32[80,128,60]{1,2,0:T(8,128)S(1)} %fusion.46, f32[80,128,60]{1,2,0:T(8,128)} %copy-done, f32[60,128]{1,0:T(8,128)S(1)} %get-tuple-element.13, f32[60,128]{1,0:T(8,128)S(1)} %get-tuple-element.14), kind=kOutput, calls=%fused_computation.20 | convolution fusion | flops 194321792 | bytes 5975040 | tf_op jit(solution)/shard_map/jm,ckm->cjk/dot_general | solution.py:41
  61.9 2.0 reshape.83
  65.6 8.6 %copy.74 = f32[2,8,10,1536]{2,1,0,3:T(8,128)} copy(f32[2,8,10,1536]{3,2,1,0:T(8,128)S(1)} %pad_maximum_fusion) | data formatting | bytes 1966080 | tf_op jit(solution)/shard_map/stack | solution.py:69
  74.3 13.2 %reshape.84 = f32[64,1,3840]{2,1,0:T(1,128)} reshape(f32[1536,2,8,10]{3,2,1,0:T(8,128)} %bitcast.72) | data formatting | bytes 1966080
  87.4 19.6 %all-to-all-start = ((f32[64,1,3840]{2,1,0:T(1,128)}), f32[64,1,3840]{2,1,0:T(1,128)S(1)}, u32[]{:S(2)}, u32[]{:S(2)}) async-start(f32[64,1,3840]{2,1,0:T(1,128)} %reshape.84), calls=%async_computation | async-start | bytes 1966080 | tf_op jit(solution)/shard_map/all_to_all | solution.py:82
  107.1 25.0 %all-to-all-done = f32[64,1,3840]{2,1,0:T(1,128)S(1)} async-done(((f32[64,1,3840]{2,1,0:T(1,128)}), f32[64,1,3840]{2,1,0:T(1,128)S(1)}, u32[]{:S(2)}, u32[]{:S(2)}) %all-to-all-start) | async-done | bytes 983072 | tf_op jit(solution)/shard_map/all_to_all | solution.py:82
  132.6 3.0 %reduce = f32[64,3840]{1,0:T(8,128)S(1)} reduce(f32[64,1,3840]{2,1,0:T(1,128)S(1)} %all-to-all-done, f32[]{:T(128)} %broadcast.109), dimensions={1}, to_apply=%all_to_all.13.reduce_sub_computation | reduce | bytes 1966084 | tf_op jit(solution)/shard_map/all_to_all | solution.py:82
  135.6 15.3 %reshape.85 = f32[1536,2,8,10]{3,2,1,0:T(8,128)} reshape(f32[64,3840]{1,0:T(8,128)S(1)} %reduce) | data formatting | bytes 1966080
  150.8 9.4 %copy.76 = f32[2,8,10,64,24]{3,4,2,1,0:T(8,128)S(1)} copy(f32[2,8,10,64,24]{2,1,0,4,3:T(8,128)} %bitcast.70) | data formatting | bytes 1966080 | tf_op jit(solution)/shard_map/all_to_all | solution.py:82
  160.2 11.0 %copy.77 = f32[2,8,64,10,24]{4,1,3,2,0:T(8,128)} copy(f32[2,8,64,10,24]{3,1,0,4,2:T(8,128)} %bitcast.71) | data formatting | bytes 1966080 | tf_op jit(solution)/shard_map/all_to_all | solution.py:82
  171.3 7.4 %fusion.10 = f32[2,8,64,24]{2,3,1,0:T(8,128)} fusion(f32[2,8,640,24]{3,1,2,0:T(8,128)} %bitcast.73, s32[640]{0:T(1024)S(1)} %iota_add_fusion, s32[64]{0:T(128)S(1)} %copy-done.5), kind=kOutput, calls=%fused_computation.23 | convolution fusion | flops 188784640 | bytes 1084160 | tf_op jit(solution)/shard_map/sr,gtrf->gtsf/dot_general | solution.py:77
  178.7 1.4 fusion.107
  180.1 4.1 %copy.80 = f32[2,8,640,24]{2,1,0,3:T(8,128)} copy(f32[2,8,640,24]{3,1,2,0:T(8,128)} %bitcast.74) | data formatting | bytes 1966080 | tf_op jit(solution)/shard_map/all_to_all | solution.py:82
  184.2 2.0 copy.82
  186.2 0.9 copy.84
  187.1 2.3 copy.81
  189.4 1.6 copy.83
  191.0 60.0 %all-reduce.2.cloned.1.call-done = f32[2,8,64,24]{2,3,1,0:T(8,128)} async-done(((f32[2,8,64,24]{2,3,1,0:T(8,128)}), f32[2,8,64,24]{2,3,1,0:T(8,128)}) %all-reduce.2.cloned.1.call-update) | async-done | bytes 98320 | tf_op jit(solution)/shard_map/psum | solution.py:86
  251.0 4.6 %convolution_bitcast_fusion.1 = f32[24,1,64,640]{3,2,0,1:T(8,128)S(1)} fusion(f32[2,8,640,24]{2,1,0,3:T(8,128)} %copy.80, f32[2,8,64,24]{2,3,1,0:T(8,128)} %all-reduce.2.cloned.1.call-done), kind=kOutput, calls=%fused_computation.17 | convolution fusion | flops 188743680 | bytes 5013504 | tf_op jit(solution)/shard_map/ikev,ikwv->vew/dot_general | solution.py:88
  255.7 3.3 %convolution_bitcast_fusion = f32[24,1,64,640]{3,2,0,1:T(8,128)S(1)} fusion(f32[1,8,640,24]{2,1,0,3:T(8,128)S(1)} %copy.84, f32[1,8,640,24]{2,1,0,3:T(8,128)S(1)} %copy-done.2, f32[2,8,64,24]{2,3,1,0:T(8,128)S(1)} %copy-done.3), kind=kOutput, calls=%fused_computation.16 | convolution fusion | flops 188989440 | bytes 5013504 | tf_op jit(solution)/shard_map/ikev,ikwv->vew/dot_general | solution.py:89
  258.9 1.0 fusion
  259.9 2.4 copy.86
  (25 shorter events, 2.4 us)
Async XLA Ops:
  18.0 4.4 %copy-start.1 = (f32[80,60,128]{2,1,0:T(8,128)S(1)}, f32[80,60,128]{2,1,0:T(8,128)}, u32[]{:S(2)}) copy-start(f32[80,60,128]{2,1,0:T(8,128)} %reshape_reshape.3) | copy-start | bytes 7372804
  24.9 16.2 %copy-start = (f32[80,128,60]{1,2,0:T(8,128)}, f32[80,128,60]{1,2,0:T(8,128)S(1)}, u32[]{:S(2)}) copy-start(f32[80,128,60]{1,2,0:T(8,128)S(1)} %fusion.44) | copy-start | bytes 7372804
  51.5 12.4 %copy-start.4 = (s32[33]{0:T(128)S(1)}, s32[33]{0:T(128)}, u32[]{:S(2)}) copy-start(s32[33]{0:T(128)} %param.5) | copy-start | bytes 400
  87.4 44.7 %all-to-all-start = ((f32[64,1,3840]{2,1,0:T(1,128)}), f32[64,1,3840]{2,1,0:T(1,128)S(1)}, u32[]{:S(2)}, u32[]{:S(2)}) async-start(f32[64,1,3840]{2,1,0:T(1,128)} %reshape.84), calls=%async_computation | async-start | bytes 1966080 | tf_op jit(solution)/shard_map/all_to_all | solution.py:82
  107.0 144.0 %all-reduce.2.cloned.1.call-start = ((), (), s32[]{:S(2)}) async-start(), calls=%async_computation.1 | async-start | bytes 393216 | tf_op jit(solution)/shard_map/psum | solution.py:86
  160.2 11.1 %copy-start.5 = (s32[64]{0:T(128)S(1)}, s32[64]{0:T(128)}, u32[]{:S(2)}) copy-start(s32[64]{0:T(128)} %param.4) | copy-start | bytes 772
  191.0 64.7 %copy-start.2 = (f32[1,8,640,24]{2,1,0,3:T(8,128)S(1)}, f32[1,8,640,24]{2,1,0,3:T(8,128)}, u32[]{:S(2)}) copy-start(f32[1,8,640,24]{2,1,0,3:T(8,128)} %copy.83) | copy-start | bytes 1474564
  251.0 4.6 %copy-start.3 = (f32[2,8,64,24]{2,3,1,0:T(8,128)S(1)}, f32[2,8,64,24]{2,3,1,0:T(8,128)}, u32[]{:S(2)}) copy-start(f32[2,8,64,24]{2,3,1,0:T(8,128)} %all-reduce.2.cloned.1.call-done) | copy-start | bytes 294916
Sparse Core Ops, SparseCore 0:
  178.8 72.1 all-reduce.1
where the time goes:
time: 274 us; the launch traced here: 269 us
  waiting for transfers between devices  85 us (31%)
  local copies, waits for them, and re-layouts  83.5 us (30%)
  matrix products  58.2 us (21%)
  starting transfers between devices  19.6 us (7%)
  between operations  13.8 us (5%)
  other arithmetic  9.18 us (3%)
    psum x1, waiting for transfers between devices, shards(): source_list = lax.psum(picked, 'rblk')  60 us
    unnamed x14, local copies, waits for them, and re-layouts  28.4 us
    all_to_all x4, local copies, waits for them, and re-layouts, shards(): lax.all_to_all(local_part, 'chan', split_axis=3, concat_axis=2, tiled=True)  25 us
    all_to_all x1, waiting for transfers between devices, shards(): lax.all_to_all(local_part, 'chan', split_axis=3, concat_axis=2, tiled=True)  25 us
    all_to_all x1, starting transfers between devices, shards(): lax.all_to_all(local_part, 'chan', split_axis=3, concat_axis=2, tiled=True)  19.6 us
    dot_general x1, matrix products, forward_bins(): jnp.einsum('jm,ckm->cjk', sin_second, twist_re, precision=peak_value)  10.5 us
    another operation x3, local copies, waits for them, and re-layouts, spectra_block(): jnp.stack([white_re.reshape(seg_count, chan_count, NF), white_im.reshape(...  8.76 us
    dot_general x1, matrix products, forward_bins(): jnp.einsum('jm,ckm->cjk', cos_second, twist_im, precision=peak_value)  8.75 us
  transfers between devices with their start and end apart: 2, of which 2 were waited for; matrix products, arithmetic and copies ran while one was open for 5% of the time, Pallas kernels for 0%

commit v1 on v0

v1 whole, which is shorter than its diff:
```python
import functools

import jax
import jax.numpy as jnp
import numpy as np
from jax import lax
from jax.experimental import pallas as pl
from jax.experimental.pallas import tpu as pltpu
from jax.sharding import PartitionSpec as P

SEG = 8
NSAMP = 7680
F_LOW = 7
NF = 1536
NB = 32
NS = 64
NDEV = 64
NBIN = 24
CH = 10
HOP = NSAMP // NBIN
HPAD = 384
GROUPS = 3
ROWS = 32
RECV = NDEV * CH

EPS = 1e-06
CLIP = 2.0
F32 = jnp.float32
BF16 = jnp.bfloat16
NT = (((1,), (1,)), ((), ()))
VMEM_LIMIT = 48 * 1024 * 1024


def split_np(values):
    hi = values.astype(jnp.bfloat16)
    lo = (values - hi.astype(np.float64)).astype(jnp.bfloat16)
    return hi, lo


@functools.lru_cache(maxsize=None)
def tables():
    m = np.arange(HPAD)
    inside = (m < HOP).astype(np.float64)
    s = np.arange(NBIN) + F_LOW
    angle = 2.0 * np.pi * ((s[:, None] * m[None, :]) % NSAMP) / NSAMP
    twiddle = np.stack([np.cos(angle) * inside, -np.sin(angle) * inside], axis=1)
    d = np.arange(NDEV)
    angle = 2.0 * np.pi * ((m[:, None] * d[None, :]) % HOP) / HOP
    cos, sin = np.cos(angle) * inside[:, None], np.sin(angle) * inside[:, None]
    w = np.concatenate(
        [np.concatenate([cos, -sin], axis=1), np.concatenate([sin, cos], axis=1)], axis=0
    )
    w_hi, w_lo = split_np(w)
    return (
        twiddle.reshape(2 * NBIN, HPAD).astype(np.float32),
        np.concatenate([w_hi, w_lo], axis=1),
    )


def split(x):
    hi = x.astype(BF16)
    lo = (x - hi.astype(F32)).astype(BF16)
    return hi, lo


def real_dft8(x):
    r = np.float32(np.sqrt(0.5))
    e0, e1, e2, e3 = x[0] + x[4], x[1] + x[5], x[2] + x[6], x[3] + x[7]
    f0, f1, f2, f3 = x[0] - x[4], x[1] - x[5], x[2] - x[6], x[3] - x[7]
    g0, g1 = e0 + e2, e1 + e3
    p, q = (f1 - f3) * r, (f1 + f3) * r
    return [
        (g0 + g1, None),
        (f0 + p, -(f2 + q)),
        (e0 - e2, e3 - e1),
        (f0 - p, f2 - q),
        (g0 - g1, None),
    ]


def real_dft24(x):
    h = np.float32(np.sqrt(3.0) / 2.0)
    parts = [real_dft8([x[(8 * a + 3 * b) % 24] for b in range(8)]) for a in range(3)]
    out = [None] * 24

    def put(ka, kb, re, im):
        k = (16 * ka + 9 * kb) % 24
        out[k] = (re, im)
        if (24 - k) % 24 != k:
            out[24 - k] = (re, None if im is None else -im)

    for kb in range(5):
        (r0, i0), (r1, i1), (r2, i2) = (parts[a][kb] for a in range(3))
        sr, dr = r1 + r2, (r1 - r2) * h
        cr = r0 - 0.5 * sr
        if i0 is None:
            put(0, kb, r0 + sr, None)
            put(1, kb, cr, -dr)
        else:
            si, di = i1 + i2, (i1 - i2) * h
            ci = i0 - 0.5 * si
            put(0, kb, r0 + sr, i0 + si)
            put(1, kb, cr + di, ci - dr)
            put(2, kb, cr - di, ci + dr)
    return out


def spectra_kernel(rec_ref, lo_ref, hi_ref, tw_ref, w_ref, out_ref, x_ref, a_ref, z_ref, p_ref):
    lane = lax.broadcasted_iota(jnp.int32, (SEG, 128), 1)
    low_half = lane < 64

    for seg in range(SEG):
        for n in range(NSAMP // 128):
            x_ref[pl.ds(n * 128 + seg * 16, CH), :] = rec_ref[seg, :, pl.ds(n * 128, 128)].astype(F32)

    def channel(i, carry):
        def tile(n):
            return x_ref[pl.ds(n * 128 + i, SEG, stride=16), :]

        total = [None] * 4
        for n in range(NSAMP // 128):
            v = tile(n)
            total[n % 4] = v * v if total[n % 4] is None else total[n % 4] + v * v
        power = jnp.sum((total[0] + total[1]) + (total[2] + total[3]), axis=1, keepdims=True)
        bound = jnp.broadcast_to(CLIP * jnp.sqrt(power * (1.0 / NSAMP) + EPS), (SEG, 128))

        def clipped(n):
            return jnp.minimum(jnp.maximum(tile(n), -bound), bound)

        for q in range(3):
            x = []
            for a in range(NBIN):
                first = (a // 2) * 5
                if a % 2 == 0:
                    x.append(clipped(first + q))
                else:
                    left = pltpu.roll(clipped(first + 2 + q), 64, 1)
                    if q < 2:
                        right = pltpu.roll(clipped(first + 3 + q), 64, 1)
                        left = jnp.where(low_half, left, right)
                    x.append(left)
            y = real_dft24(x)
            for pair in range(NBIN // 2):
                res, ims = [], []
                for s in (2 * pair, 2 * pair + 1):
                    re, im = y[(s + F_LOW) % 24]
                    c = tw_ref[pl.ds(2 * s, 1), pl.ds(q * 128, 128)]
                    e = tw_ref[pl.ds(2 * s + 1, 1), pl.ds(q * 128, 128)]
                    if im is None:
                        res.append(re * c)
                        ims.append(re * e)
                    else:
                        res.append(re * c - im * e)
                        ims.append(re * e + im * c)
                for part, values in enumerate((res, ims)):
                    hi, lo = split(jnp.concatenate(values, axis=0))
                    a_ref[0, pl.ds(pair * 16, 16), pl.ds(part * HPAD + q * 128, 128)] = hi
                    a_ref[1, pl.ds(pair * 16, 16), pl.ds(part * HPAD + q * 128, 128)] = lo
        both = jnp.dot(a_ref[0], w_ref[...], preferred_element_type=F32)
        z = both[:, :128] + both[:, 128:]
        z = z + jnp.dot(a_ref[1], w_ref[:, :128], preferred_element_type=F32)
        row = pl.multiple_of(i * NBIN * SEG, NBIN * SEG)
        z_ref[pl.ds(row, NBIN * SEG), :] = z
        top = pl.multiple_of(i * SEG, SEG)
        for s in range(NBIN):
            v = z[s * SEG : (s + 1) * SEG]
            p_ref[pl.ds(top, SEG), pl.ds(s * 128, 128)] = v * v
        return carry

    lax.fori_loop(0, CH, channel, 0)

    shape = (NB, NBIN * 128)
    at = lax.broadcasted_iota(jnp.int32, shape, 1)
    bin_index = (at % 64) * NBIN + at // 128
    low, high = lo_ref[...], hi_ref[...]
    member = ((bin_index >= low) & (bin_index < high)).astype(F32).astype(BF16)
    p_hi, p_lo = split(p_ref[...])
    band = lax.dot_general(p_hi, member, NT, preferred_element_type=F32)
    band = band + lax.dot_general(p_lo, member, NT, preferred_element_type=F32)
    widths = jnp.sum(member.astype(F32), axis=1, keepdims=True) * 0.5
    eye = lax.broadcasted_iota(jnp.int32, (NB, NB), 0) == lax.broadcasted_iota(jnp.int32, (NB, NB), 1)
    widths = jnp.sum(jnp.where(eye, widths, 0.0), axis=0, keepdims=True)
    scale = lax.rsqrt(band / widths + EPS)
    s_hi = scale.astype(BF16)
    rest = scale - s_hi.astype(F32)
    s_mid, s_lo = split(rest)
    per_bin = jnp.dot(s_hi, member, preferred_element_type=F32)
    per_bin = per_bin + jnp.dot(s_mid, member, preferred_element_type=F32)
    per_bin = per_bin + jnp.dot(s_lo, member, preferred_element_type=F32)
    p_ref[...] = per_bin

    half64 = lax.broadcasted_iota(jnp.int32, (64, 128), 1) < 64

    def pair_of_channels(j, carry):
        for t in range(GROUPS):
            blocks = []
            for k in range(2):
                i = 2 * j + k
                z = z_ref[pl.ds(pl.multiple_of(i * NBIN * SEG, NBIN * SEG) + t * 64, 64), :]
                factor = jnp.concatenate(
                    [
                        p_ref[pl.ds(pl.multiple_of(i * SEG, SEG), SEG), pl.ds((t * 8 + u) * 128, 128)]
                        for u in range(8)
                    ],
                    axis=0,
                )
                blocks.append(z * factor)
            first, second = blocks
            upper = jnp.where(half64, first, pltpu.roll(second, 64, 1))
            lower = jnp.where(half64, pltpu.roll(first, 64, 1), second)
            turned = jnp.concatenate([upper, lower], axis=0).T
            out_ref[pl.ds(t * CH + 2 * j, NDEV, stride=ROWS), :] = turned[:64]
            out_ref[pl.ds(t * CH + 2 * j + 1, NDEV, stride=ROWS), :] = turned[64:]
        return carry

    lax.fori_loop(0, CH // 2, pair_of_channels, 0)
    for r in range(GROUPS * CH, ROWS):
        out_ref[pl.ds(r, NDEV, stride=ROWS), :] = jnp.zeros((NDEV, 128), F32)


def vmem():
    return pl.BlockSpec(memory_space=pltpu.VMEM)


def smem():
    return pl.BlockSpec(memory_space=pltpu.SMEM)


def spectra(records, band_edges):
    twiddle, w = tables()
    return pl.pallas_call(
        spectra_kernel,
        out_shape=jax.ShapeDtypeStruct((NDEV * ROWS, 128), F32),
        in_specs=[vmem()] * 5,
        out_specs=vmem(),
        scratch_shapes=[
            pltpu.VMEM((NSAMP, 128), F32),
            pltpu.VMEM((2, NBIN * SEG, 2 * HPAD), BF16),
            pltpu.VMEM((CH * NBIN * SEG, 128), F32),
            pltpu.VMEM((CH * SEG, NBIN * 128), F32),
        ],
        compiler_params=pltpu.CompilerParams(vmem_limit_bytes=VMEM_LIMIT),
        name="spectra",
    )(records, band_edges[:-1, None], band_edges[1:, None], jnp.asarray(twiddle), jnp.asarray(w))


def pick_kernel(local_ref, recv_ref, out_ref):
    def one(k, carry):
        local = local_ref[k]
        here = (local >= 0) & (local < RECV)
        place = jnp.clip(local, 0, RECV - 1)
        row = (place // CH) * ROWS + place % CH
        for t in range(GROUPS):
            v = recv_ref[pl.ds(row + t * CH, 1), :]
            out_ref[pl.ds(t * NS + k, 1), :] = jnp.where(here, v, 0.0)
        return carry

    lax.fori_loop(0, NS, one, 0)


def pick(local, received):
    return pl.pallas_call(
        pick_kernel,
        out_shape=jax.ShapeDtypeStruct((GROUPS * NS, 128), F32),
        in_specs=[smem(), vmem()],
        out_specs=vmem(),
        name="pick",
    )(local, received)


def pack_kernel(recv_ref, out_ref, dense_ref):
    for t in range(GROUPS):
        for i in range(CH):
            dense_ref[pl.ds(i, NDEV, stride=CH), :] = recv_ref[pl.ds(t * CH + i, NDEV, stride=ROWS), :]
        hi, lo = split(dense_ref[...])
        out_ref[t, :, pl.ds(0, 128)] = hi
        out_ref[t, :, pl.ds(128, 128)] = lo


def pack(received):
    return pl.pallas_call(
        pack_kernel,
        out_shape=jax.ShapeDtypeStruct((GROUPS, RECV, 256), BF16),
        in_specs=[vmem()],
        out_specs=vmem(),
        scratch_shapes=[pltpu.VMEM((RECV, 128), F32)],
        cost_estimate=pl.CostEstimate(flops=2000000, bytes_accessed=4000000, transcendentals=0),
        compiler_params=pltpu.CompilerParams(vmem_limit_bytes=VMEM_LIMIT),
        name="pack",
    )(received)


def correlate_kernel(src_ref, recv_ref, out_ref, left_ref, small_ref):
    s = src_ref[0]
    for b in range(1, src_ref.shape[0]):
        s = s + src_ref[b]
    s = s * (1.0 / SEG)
    lane = lax.broadcasted_iota(jnp.int32, (NS, 128), 1)
    turned = pltpu.roll(s, 64, 1)
    turned = jnp.where(lane < 64, -turned, turned)
    both = jnp.concatenate([s, turned], axis=0)
    hi, lo = split(both)
    which = lax.broadcasted_iota(jnp.int32, (2 * NS, 128), 1) // SEG % 8
    none = jnp.zeros_like(hi)
    for u in range(8):
        rows = pl.ds(u * 2 * NS, 2 * NS)
        chosen = jnp.where(which == u, hi, none)
        left_ref[rows, pl.ds(0, 128)] = chosen
        left_ref[rows, pl.ds(128, 128)] = chosen
        small_ref[rows, :] = jnp.where(which == u, lo, none)
    right = recv_ref[0]
    result = lax.dot_general(left_ref[...], right, NT, preferred_element_type=F32)
    result = result + lax.dot_general(small_ref[...], right[:, :128], NT, preferred_element_type=F32)
    out_ref[...] = result.astype(BF16).reshape(out_ref.shape)


def correlate(sources, packed):
    blocks = sources.shape[0]
    return pl.pallas_call(
        correlate_kernel,
        grid=(GROUPS,),
        out_shape=jax.ShapeDtypeStruct((NBIN, 2, NS, RECV), BF16),
        in_specs=[
            pl.BlockSpec((blocks, NS, 128), lambda t: (0, t, 0)),
            pl.BlockSpec((1, RECV, 256), lambda t: (t, 0, 0)),
        ],
        out_specs=pl.BlockSpec((8, 2, NS, RECV), lambda t: (t, 0, 0, 0)),
        scratch_shapes=[
            pltpu.VMEM((16 * NS, 256), BF16),
            pltpu.VMEM((16 * NS, 128), BF16),
        ],
        compiler_params=pltpu.CompilerParams(vmem_limit_bytes=VMEM_LIMIT),
        name="correlate",
    )(sources, packed)


def shards(records, source_index, band_edges):
    local = source_index - lax.axis_index("rblk") * RECV
    sent = spectra(records, band_edges)
    received = lax.all_to_all(sent, "chan", split_axis=0, concat_axis=0, tiled=True)
    picked = pick(local, received)
    sources = lax.all_gather(picked, "rblk", axis=0, tiled=False)
    packed = pack(received)
    return correlate(sources, packed)


def solution(mesh):
    return jax.shard_map(
        shards,
        mesh=mesh,
        in_specs=(P(None, ("rblk", "chan"), None), P(), P()),
        out_specs=P("chan", None, None, "rblk"),
        check_vma=False,
    )
```

time: 274 us -> 92.4 us (0.34); the launches traced: 269 us -> 92.2 us
  local copies, waits for them, and re-layouts: 83.5 us -> 2.75 us
  waiting for transfers between devices: 85 us -> 25.2 us
  matrix products: 58.2 us -> 0 us
  blocking collectives: 0 us -> 24.1 us
  Pallas kernels: 0 us -> 19.9 us
  between operations: 13.8 us -> 0.06 us
  other arithmetic: 9.18 us -> 0.54 us
    psum x1 -> x0, waiting for transfers between devices: 60 us -> none  [shards(): source_list = lax.psum(picked, 'rblk')]
    dot_general x11 -> x0, matrix products: 58.2 us -> none  [the longest x1 10.5 us: forward_bins(): jnp.einsum('jm,ckm->cjk', sin_second, twist_re, precision=peak_value)]
    unnamed x14 -> x9, local copies, waits for them, and re-layouts: 28.4 us -> 1.77 us
    all_to_all x4 -> x0, local copies, waits for them, and re-layouts: 25 us -> none  [shards(): lax.all_to_all(local_part, 'chan', split_axis=3, concat_axis=2, tiled=True)]
    all_gather x0 -> x1, blocking collectives: none -> 24.1 us  [shards(): sources = lax.all_gather(picked, 'rblk', axis=0, tiled=False)]
    pallas_call x0 -> x4, Pallas kernels: none -> 19.9 us  [the longest x1 11.7 us: spectra(): pl.pallas_call(spectra_kernel, out_shape=jax.ShapeDtypeStruct((NDEV * ROW...]
    another operation x4 -> x0, local copies, waits for them, and re-layouts: 13.5 us -> none  [the longest x3 8.76 us: spectra_block(): jnp.stack([white_re.reshape(seg_count, chan_count, NF), white_im.reshape(...]
    reshape x2 -> x0, local copies, waits for them, and re-layouts: 3.96 us -> none  [the longest x1 1.98 us: forward_bins(): flat_re = final_re.reshape(row_count, top_rows * TP)[:, F_LOW:F_LOW + NF]]
  transfers between devices with their start and end apart: 2 -> 1, of which waited for: 2 -> 1; matrix products, arithmetic and copies ran while one was open for 5% -> 1% of each run, Pallas kernels for 0% -> 0%
where the time goes in v1:
time: 92.4 us; the launch traced here: 92.2 us
  waiting for transfers between devices  25.2 us (27%)
  blocking collectives  24.1 us (26%)
  Pallas kernels  19.9 us (22%)
  starting transfers between devices  19.6 us (21%)
  local copies, waits for them, and re-layouts  2.75 us (3%)
    all_to_all x1, waiting for transfers between devices, shards(): lax.all_to_all(sent, 'chan', split_axis=0, concat_axis=0, tiled=True)  25.2 us
    all_gather x1, blocking collectives, shards(): sources = lax.all_gather(picked, 'rblk', axis=0, tiled=False)  24.1 us
    all_to_all x1, starting transfers between devices, shards(): lax.all_to_all(sent, 'chan', split_axis=0, concat_axis=0, tiled=True)  19.6 us
    pallas_call x1, Pallas kernels, spectra(): pl.pallas_call(spectra_kernel, out_shape=jax.ShapeDtypeStruct((NDEV * ROW...  11.7 us
    pallas_call x1, Pallas kernels, correlate(): pl.pallas_call(correlate_kernel, grid=(GROUPS,), out_shape=jax.ShapeDtype...  4.17 us
    pallas_call x1, Pallas kernels, pick(): pl.pallas_call(pick_kernel, out_shape=jax.ShapeDtypeStruct((GROUPS * NS,...  3.15 us
  transfers between devices with their start and end apart: 1, of which 1 were waited for; matrix products, arithmetic and copies ran while one was open for 1% of the time, Pallas kernels for 0%

profile of v1, /device:TPU:1, one launch (start us, length us, event | category | flops | bytes accessed | tf_op | source)
XLA Modules:
  0.0 92.2 jit_solution(7745815314694371865)
XLA Ops:
  0.0 0.0 copy-start.1
  0.0 0.0 copy-start.2
  0.0 0.8 slice_bitcast_fusion
  0.8 0.1 copy.8.hi_ref
  0.9 0.1 copy.7.lo_ref
  1.0 1.7 %copy.6.rec_ref = bf16[8,10,7680]{2,1,0:T(8,128)(2,1)S(1)} copy(bf16[8,10,7680]{2,0,1:T(8,128)(2,1)} %param.5) | data formatting | bytes 2457600 | tf_op args[0]
  2.7 0.0 copy-done.1
  2.7 0.0 copy-done.2
  2.7 0.0 copy-start.3
  2.7 11.7 %spectra.1 = f32[2048,128]{1,0:T(8,128)} custom-call(bf16[8,10,7680]{2,1,0:T(8,128)(2,1)S(1)} %copy.6.rec_ref, s32[32,1]{1,0:T(8,128)S(1)} %copy.7.lo_ref, s32[32,1]{1,0:T(8,128)S(1)} %copy.8.hi_ref, f32[48,384]{1,0:T(8,128)S(1)} %copy-done.2, bf16[768,256]{1,0:T(8,128)(2,1)S(1)} %copy-done.1), custom_call_target="tpu_custom_call" | custom-call | tf_op jit(solution)/shard_map/spectra/pallas_call | solution.py:231
  14.4 19.6 %all-to-all-start = ((f32[64,32,128]{2,1,0:T(8,128)}), f32[64,32,128]{2,1,0:T(8,128)S(1)}, u32[]{:S(2)}, u32[]{:S(2)}) async-start(f32[64,32,128]{2,1,0:T(8,128)} %bitcast.2), calls=%async_computation | async-start | bytes 2097152 | tf_op jit(solution)/shard_map/all_to_all | solution.py:340
  34.0 0.0 copy-done.3
  34.0 0.5 broadcast_subtract_fusion.local_ref
  34.5 25.2 %all-to-all-done = f32[64,32,128]{2,1,0:T(8,128)S(1)} async-done(((f32[64,32,128]{2,1,0:T(8,128)}), f32[64,32,128]{2,1,0:T(8,128)S(1)}, u32[]{:S(2)}, u32[]{:S(2)}) %all-to-all-start) | async-done | bytes 1048608 | tf_op jit(solution)/shard_map/all_to_all | solution.py:340
  59.8 0.0 copy-start
  59.8 0.9 pack.1.recv_ref
  60.7 0.1 copy-done
  60.7 3.2 %pick.1 = f32[192,128]{1,0:T(8,128)} custom-call(s32[64]{0:T(128)} %broadcast_subtract_fusion.local_ref, f32[2048,128]{1,0:T(8,128)} %bitcast.8), custom_call_target="tpu_custom_call" | custom-call | tf_op jit(solution)/shard_map/pick/pallas_call | solution.py:262
  63.9 24.1 %all-gather = f32[1536,128]{1,0:T(8,128)S(1)} all-gather(f32[192,128]{1,0:T(8,128)} %pick.1), channel_id=2, replica_groups=mesh['chan'=64,'rblk'=8] {'rblk'}, dimensions={0}, use_global_device_ids=true | all-gather | bytes 884736 | tf_op jit(solution)/shard_map/all_gather | solution.py:342
  88.0 4.2 %correlate.1 = bf16[24,2,64,640]{3,2,1,0:T(8,128)(2,1)} custom-call(f32[8,192,128]{2,1,0:T(8,128)S(1)} %bitcast.9, bf16[3,640,256]{2,1,0:T(8,128)(2,1)S(1)} %pack.1.recv_ref), custom_call_target="tpu_custom_call" | custom-call | tf_op jit(solution)/shard_map/correlate/pallas_call | solution.py:319
Async XLA Ops:
  0.0 2.7 %copy-start.1 = (bf16[768,256]{1,0:T(8,128)(2,1)S(1)}, bf16[768,256]{1,0:T(8,128)(2,1)}, u32[]{:S(2)}) copy-start(bf16[768,256]{1,0:T(8,128)(2,1)} %constant.11.clone.w_ref) | copy-start | bytes 1179652
  0.0 2.7 %copy-start.2 = (f32[48,384]{1,0:T(8,128)S(1)}, f32[48,384]{1,0:T(8,128)}, u32[]{:S(2)}) copy-start(f32[48,384]{1,0:T(8,128)} %constant.10.clone.tw_ref) | copy-start | bytes 221188
  2.7 31.3 %copy-start.3 = (s32[64]{0:T(128)S(1)}, s32[64]{0:T(128)}, u32[]{:S(2)}) copy-start(s32[64]{0:T(128)} %param.6) | copy-start | bytes 772
  14.4 45.4 %all-to-all-start = ((f32[64,32,128]{2,1,0:T(8,128)}), f32[64,32,128]{2,1,0:T(8,128)S(1)}, u32[]{:S(2)}, u32[]{:S(2)}) async-start(f32[64,32,128]{2,1,0:T(8,128)} %bitcast.2), calls=%async_computation | async-start | bytes 2097152 | tf_op jit(solution)/shard_map/all_to_all | solution.py:340
  59.8 1.0 %copy-start = (f32[64,32,128]{2,1,0:T(8,128)}, f32[64,32,128]{2,1,0:T(8,128)S(1)}, u32[]{:S(2)}) copy-start(f32[64,32,128]{2,1,0:T(8,128)S(1)} %all-to-all-done) | copy-start | bytes 3145732

commit v2 on v1

v2 whole, which is shorter than its diff:
```python
import functools

import jax
import jax.numpy as jnp
import numpy as np
from jax import lax
from jax.experimental import pallas as pl
from jax.experimental.pallas import tpu as pltpu
from jax.sharding import PartitionSpec as P

SEG = 8
NSAMP = 7680
F_LOW = 7
NF = 1536
NB = 32
NS = 64
NDEV = 64
NBIN = 24
CH = 10
HOP = NSAMP // NBIN
HPAD = 384
GROUPS = 3
ROWS = GROUPS * CH
ROOM = 20
RECV = NDEV * CH

EPS = 1e-06
CLIP = 2.0
F32 = jnp.float32
BF16 = jnp.bfloat16
NT = (((1,), (1,)), ((), ()))
VMEM_LIMIT = 40 * 1024 * 1024
FULL_VMEM = 60 * 1024 * 1024


def split_np(values):
    hi = values.astype(jnp.bfloat16)
    lo = (values - hi.astype(np.float64)).astype(jnp.bfloat16)
    return hi, lo


@functools.lru_cache(maxsize=None)
def tables():
    m = np.arange(HPAD)
    inside = (m < HOP).astype(np.float64)
    s = np.arange(NBIN) + F_LOW
    angle = 2.0 * np.pi * ((s[:, None] * m[None, :]) % NSAMP) / NSAMP
    twiddle = np.stack([np.cos(angle) * inside, -np.sin(angle) * inside], axis=1)
    d = np.arange(NDEV)
    angle = 2.0 * np.pi * ((m[:, None] * d[None, :]) % HOP) / HOP
    cos, sin = np.cos(angle) * inside[:, None], np.sin(angle) * inside[:, None]
    w = np.stack([np.concatenate([cos, -sin], axis=1), np.concatenate([sin, cos], axis=1)])
    w = w.reshape(2, 3, 128, 2 * NDEV).transpose(1, 0, 2, 3).reshape(2 * HPAD, 2 * NDEV)
    w_hi, w_lo = split_np(w)
    return (
        twiddle.reshape(2 * NBIN, HPAD).astype(np.float32),
        np.concatenate([w_hi, w_lo], axis=1),
    )


def split(x):
    hi = x.astype(BF16)
    lo = (x - hi.astype(F32)).astype(BF16)
    return hi, lo


def real_dft8(x):
    r = np.float32(np.sqrt(0.5))
    e0, e1, e2, e3 = x[0] + x[4], x[1] + x[5], x[2] + x[6], x[3] + x[7]
    f0, f1, f2, f3 = x[0] - x[4], x[1] - x[5], x[2] - x[6], x[3] - x[7]
    g0, g1 = e0 + e2, e1 + e3
    p, q = (f1 - f3) * r, (f1 + f3) * r
    return [
        (g0 + g1, None),
        (f0 + p, -(f2 + q)),
        (e0 - e2, e3 - e1),
        (f0 - p, f2 - q),
        (g0 - g1, None),
    ]


def real_dft24(x):
    h = np.float32(np.sqrt(3.0) / 2.0)
    parts = [real_dft8([x[(8 * a + 3 * b) % 24] for b in range(8)]) for a in range(3)]
    out = [None] * 24

    def put(ka, kb, re, im):
        k = (16 * ka + 9 * kb) % 24
        out[k] = (re, im)
        if (24 - k) % 24 != k:
            out[24 - k] = (re, None if im is None else -im)

    for kb in range(5):
        (r0, i0), (r1, i1), (r2, i2) = (parts[a][kb] for a in range(3))
        sr, dr = r1 + r2, (r1 - r2) * h
        cr = r0 - 0.5 * sr
        if i0 is None:
            put(0, kb, r0 + sr, None)
            put(1, kb, cr, -dr)
        else:
            si, di = i1 + i2, (i1 - i2) * h
            ci = i0 - 0.5 * si
            put(0, kb, r0 + sr, i0 + si)
            put(1, kb, cr + di, ci - dr)
            put(2, kb, cr - di, ci + dr)
    return out


def spectra_kernel(
    rec_hbm, edge_hbm, tw_hbm, w_hbm, out_ref,
    rec_ref, even_ref, odd_ref, z_ref, p_ref, m_ref, tw_ref, w_ref, edge_ref, rec_sems, sems,
):
    def fetch(i):
        return pltpu.make_async_copy(rec_hbm.at[i], rec_ref.at[i], rec_sems.at[i])

    small = [(edge_hbm, edge_ref), (tw_hbm, tw_ref), (w_hbm, w_ref)]
    copies = [pltpu.make_async_copy(a, b, sems.at[k]) for k, (a, b) in enumerate(small)]
    copies[0].start()
    fetch(0).start()
    copies[1].start()
    copies[2].start()
    for i in range(1, CH):
        fetch(i).start()

    copies[0].wait()
    shape = (NB, 128)
    row = lax.broadcasted_iota(jnp.int32, shape, 0)
    low, high = jnp.zeros(shape, jnp.int32), jnp.zeros(shape, jnp.int32)
    for k in range(NB):
        low = jnp.where(row == k, edge_ref[k], low)
        high = jnp.where(row == k, edge_ref[k + 1], high)
    widths = (high - low).astype(F32)
    eye = row == lax.broadcasted_iota(jnp.int32, shape, 1)
    widths = jnp.sum(jnp.where(eye, widths, 0.0), axis=0, keepdims=True)[:, :NB]
    start = (lax.broadcasted_iota(jnp.int32, shape, 1) & (NDEV - 1)) * NBIN
    for s in range(NBIN):
        inside = (start + s >= low) & (start + s < high)
        m_ref[:, pl.ds(s * 128, 128)] = jnp.where(inside, 1.0, 0.0).astype(BF16)
    copies[1].wait()
    copies[2].wait()

    lane = lax.broadcasted_iota(jnp.int32, (SEG, 128), 1)
    low_half = lane < 64

    def transform(i, a_ref):
        def tile(n):
            return rec_ref[i, :, pl.ds(n * 128, 128)].astype(F32)

        total = [None] * 4
        for n in range(NSAMP // 128):
            v = tile(n)
            total[n % 4] = v * v if total[n % 4] is None else total[n % 4] + v * v
        power = jnp.sum((total[0] + total[1]) + (total[2] + total[3]), axis=1, keepdims=True)
        bound = jnp.broadcast_to(CLIP * jnp.sqrt(power * (1.0 / NSAMP) + EPS), (SEG, 128))

        def clip(v):
            return jnp.minimum(jnp.maximum(v, -bound), bound)

        for q in range(3):
            x = []
            for a in range(NBIN):
                n = (a // 2) * 5 + q
                if a % 2 == 0:
                    x.append(clip(tile(n)))
                else:
                    left = tile(n + 2)
                    right = tile(n + 3) if q < 2 else left
                    x.append(clip(pltpu.roll(jnp.where(low_half, right, left), 64, 1)))
            y = real_dft24(x)
            for pair in range(NBIN // 2):
                res, ims = [], []
                for s in (2 * pair, 2 * pair + 1):
                    re, im = y[(s + F_LOW) % 24]
                    c = tw_ref[pl.ds(2 * s, 1), pl.ds(q * 128, 128)]
                    e = tw_ref[pl.ds(2 * s + 1, 1), pl.ds(q * 128, 128)]
                    if im is None:
                        res.append(re * c)
                        ims.append(re * e)
                    else:
                        res.append(re * c - im * e)
                        ims.append(re * e + im * c)
                for part, values in enumerate((res, ims)):
                    hi, lo = split(jnp.concatenate(values, axis=0))
                    a_ref[q, 0, pl.ds(pair * 16, 16), pl.ds(part * 128, 128)] = hi
                    a_ref[q, 1, pl.ds(pair * 16, 16), pl.ds(part * 128, 128)] = lo

    def multiply(place, a_ref):
        z = None
        for q in range(3):
            depth = pl.ds(q * 256, 256)
            both = jnp.dot(a_ref[q, 0], w_ref[depth, :], preferred_element_type=F32)
            rest = jnp.dot(a_ref[q, 1], w_ref[depth, pl.ds(0, 128)], preferred_element_type=F32)
            term = (both[:, :128] + both[:, 128:]) + rest
            z = term if z is None else z + term
        z_ref[pl.ds(pl.multiple_of(place * NBIN * SEG, NBIN * SEG), NBIN * SEG), :] = z
        for s in range(NBIN):
            v = z[s * SEG : (s + 1) * SEG]
            p_ref[pl.ds(pl.multiple_of(place * SEG, SEG), SEG), pl.ds(s * 128, 128)] = v * v

    def two_channels(j, carry):
        fetch(2 * j).wait()
        fetch(2 * j + 1).wait()
        multiply(2 * j, odd_ref)
        transform(2 * j, even_ref)
        multiply(2 * j + 1, even_ref)
        transform(2 * j + 1, odd_ref)
        return carry

    lax.fori_loop(0, CH // 2, two_channels, 0)
    multiply(CH, odd_ref)

    member = m_ref[...]
    rows = CH * SEG
    power = jnp.concatenate(split(p_ref[pl.ds(SEG, rows), :]), axis=0)
    band = lax.dot_general(power, member, NT, preferred_element_type=F32)
    band = band[:rows] + band[rows:]
    scale = lax.rsqrt(band / widths + EPS)
    s_hi = scale.astype(BF16)
    rest = scale - s_hi.astype(F32)
    s_mid, s_lo = split(rest)
    scales = jnp.concatenate([s_hi, s_mid, s_lo], axis=1)
    copied = jnp.concatenate([member] * 3, axis=0)
    per_bin = jnp.dot(scales, copied, preferred_element_type=F32)
    p_ref[pl.ds(SEG, CH * SEG), :] = per_bin

    half64 = lax.broadcasted_iota(jnp.int32, (64, 128), 1) < 64
    where = [(t, i) for i in range(CH) for t in range(GROUPS)]

    def whitened(t, i):
        z = z_ref[pl.ds((i + 1) * NBIN * SEG + t * 64, 64), :]
        factor = [p_ref[pl.ds((i + 1) * SEG, SEG), pl.ds((t * 8 + u) * 128, 128)] for u in range(8)]
        return z * jnp.concatenate(factor, axis=0)

    for k in range(0, len(where), 2):
        first, second = whitened(*where[k]), whitened(*where[k + 1])
        upper = jnp.where(half64, first, pltpu.roll(second, 64, 1))
        lower = jnp.where(half64, pltpu.roll(first, 64, 1), second)
        halves = [h[u * SEG : (u + 1) * SEG] for u in range(8) for h in (upper, lower)]
        turned = jnp.concatenate(halves, axis=0).T
        for part in range(2):
            t, i = where[k + part]
            out_ref[pl.ds(t * CH + i, NDEV, stride=ROWS), :] = turned[part * 64 : part * 64 + 64]


def vmem():
    return pl.BlockSpec(memory_space=pltpu.VMEM)


def smem():
    return pl.BlockSpec(memory_space=pltpu.SMEM)


def spectra(records, band_edges):
    twiddle, w = tables()
    return pl.pallas_call(
        spectra_kernel,
        out_shape=jax.ShapeDtypeStruct((NDEV * ROWS, 128), F32),
        in_specs=[pl.BlockSpec(memory_space=pltpu.HBM)] * 4,
        out_specs=vmem(),
        scratch_shapes=[
            pltpu.VMEM((CH, SEG, NSAMP), BF16),
            pltpu.VMEM((3, 2, NBIN * SEG, 256), BF16),
            pltpu.VMEM((3, 2, NBIN * SEG, 256), BF16),
            pltpu.VMEM(((CH + 1) * NBIN * SEG, 128), F32),
            pltpu.VMEM(((CH + 1) * SEG, NBIN * 128), F32),
            pltpu.VMEM((NB, NBIN * 128), BF16),
            pltpu.VMEM(twiddle.shape, F32),
            pltpu.VMEM(w.shape, BF16),
            pltpu.SMEM((NB + 1,), jnp.int32),
            pltpu.SemaphoreType.DMA((CH,)),
            pltpu.SemaphoreType.DMA((3,)),
        ],
        compiler_params=pltpu.CompilerParams(vmem_limit_bytes=FULL_VMEM),
        name="spectra",
    )(records, band_edges, jnp.asarray(twiddle), jnp.asarray(w))


def pick_kernel(copies, rows, ordered, place_ref, recv_ref, out_ref, held_ref):
    held_ref[...] = jnp.zeros_like(held_ref)

    def one(n, carry):
        to = place_ref[0, n] if ordered else n
        held_ref[pl.ds(to * GROUPS, GROUPS), :] = recv_ref[pl.ds(place_ref[1, n], GROUPS, stride=CH), :]
        return carry

    lax.fori_loop(0, place_ref[2, 0], one, 0)
    for k in range(copies):
        out_ref[pl.ds(k * rows, rows), :] = held_ref[...]


def pick(places, received, copies, room, ordered):
    rows = room * GROUPS
    return pl.pallas_call(
        functools.partial(pick_kernel, copies, rows, ordered),
        out_shape=jax.ShapeDtypeStruct((copies * rows, 128), F32),
        in_specs=[smem(), vmem()],
        out_specs=vmem(),
        scratch_shapes=[pltpu.VMEM((rows, 128), F32)],
        compiler_params=pltpu.CompilerParams(vmem_limit_bytes=VMEM_LIMIT),
        name="pick",
    )(places, received)


def correlate_kernel(at_ref, src_ref, recv_ref, out_hbm, left_ref, right_ref, dense_ref, s_ref, out_ref, sems):
    for k in range(NS):
        s_ref[pl.ds(k * GROUPS, GROUPS), :] = src_ref[pl.ds(at_ref[k], GROUPS), :]
    lower = lax.broadcasted_iota(jnp.int32, (RECV, 128), 1) < 64
    lane = lax.broadcasted_iota(jnp.int32, (2 * NS, 128), 1)
    imag = lane[:NS] & SEG != 0
    which = lane // (2 * SEG)
    copies = []
    for t in range(GROUPS):
        for i in range(CH):
            dense_ref[t, pl.ds(i, NDEV, stride=CH), :] = recv_ref[pl.ds(t * CH + i, NDEV, stride=ROWS), :]

        hi, lo = split(dense_ref[t])
        turned = pltpu.roll(lo.astype(F32), 64, 1).astype(BF16)
        right_ref[t, 0] = jnp.where(lower, hi, turned)
        right_ref[t, 1] = jnp.where(lower, turned, hi)
        right_ref[t, 2] = hi

        s = s_ref[pl.ds(t, NS, stride=GROUPS), :] * (1.0 / SEG)
        crossed = jnp.where(imag, pltpu.roll(s, SEG, 1), -pltpu.roll(s, 128 - SEG, 1))
        hi, lo = split(jnp.concatenate([s, crossed], axis=0))
        hi, lo = hi.astype(F32), lo.astype(F32)
        hi_turned = pltpu.roll(hi, 64, 1)
        for h in range(2):
            part = 2 * t + h
            both = jnp.where((lane < 64) == (h == 0), hi, hi_turned)
            for v in range(4):
                rows = pl.ds(v * 2 * NS, 2 * NS)
                left_ref[part, rows, pl.ds(0, 128)] = jnp.where(which % 4 == v, both, 0.0).astype(BF16)
                left_ref[part, rows, pl.ds(128, 128)] = jnp.where(which == 4 * h + v, lo, 0.0).astype(BF16)
            right = jnp.concatenate([right_ref[t, h], right_ref[t, 2]], axis=1)
            result = lax.dot_general(left_ref[part], right, NT, preferred_element_type=F32)
            bins = pl.ds(4 * part, 4)
            out_ref[bins] = result.astype(BF16).reshape(4, 2, NS, RECV)
            copies.append(pltpu.make_async_copy(out_ref.at[bins], out_hbm.at[bins], sems.at[part]))
            copies[-1].start()
    for copy in copies:
        copy.wait()


def correlate(at, sources, received):
    parts = 2 * GROUPS
    return pl.pallas_call(
        correlate_kernel,
        out_shape=jax.ShapeDtypeStruct((NBIN, 2, NS, RECV), BF16),
        in_specs=[smem(), vmem(), vmem()],
        out_specs=pl.BlockSpec(memory_space=pltpu.HBM),
        scratch_shapes=[
            pltpu.VMEM((parts, 8 * NS, 256), BF16),
            pltpu.VMEM((GROUPS, 3, RECV, 128), BF16),
            pltpu.VMEM((GROUPS, RECV, 128), F32),
            pltpu.VMEM((NS * GROUPS, 128), F32),
            pltpu.VMEM((NBIN, 2, NS, RECV), BF16),
            pltpu.SemaphoreType.DMA((parts,)),
        ],
        compiler_params=pltpu.CompilerParams(vmem_limit_bytes=VMEM_LIMIT),
        name="correlate",
    )(at, sources, received)


def plan(source_index, block):
    owner, local = source_index // RECV, source_index % RECV
    number = jnp.arange(NS, dtype=jnp.int32)
    same = owner[:, None] == owner[None, :]
    rank = jnp.sum(same & (number[None, :] < number[:, None]), axis=1, dtype=jnp.int32)
    crowded = jnp.any(rank >= ROOM)
    chosen = owner == block
    to = (chosen & (rank == number[:, None]))[None]
    row = local // CH * ROWS + local % CH
    columns = jnp.stack([number, row, jnp.ones_like(row)])[:, None, :]
    places = jnp.sum(jnp.where(to, columns, 0), axis=2)
    total = jnp.sum(chosen, dtype=jnp.int32)
    places = jnp.concatenate([places[:2], jnp.broadcast_to(total, (1, NS))])
    at = GROUPS * jnp.where(crowded, number, owner * ROOM + rank)
    return places, at, crowded


def share(places, received, blocks):
    rows = pick(places, received, blocks, ROOM, False)
    flat = rows.reshape(blocks, 1, ROOM * GROUPS * 128)
    return lax.all_to_all(flat, "rblk", split_axis=0, concat_axis=0, tiled=True).reshape(rows.shape)


def share_all(places, received, blocks):
    rows = pick(places, received, 1, NS, True)
    total = jnp.sum(lax.all_gather(rows, "rblk", axis=0, tiled=False), axis=0)
    return jnp.pad(total, ((0, (blocks * ROOM - NS) * GROUPS), (0, 0)))


def shards(records, source_index, band_edges):
    blocks = lax.axis_size("rblk")
    places, at, crowded = plan(source_index, lax.axis_index("rblk"))
    sent = spectra(jnp.transpose(records, (1, 0, 2)), band_edges)
    flat = sent.reshape(NDEV, 1, ROWS * 128)
    received = lax.all_to_all(flat, "chan", split_axis=0, concat_axis=0, tiled=True).reshape(sent.shape)
    sources = lax.cond(
        crowded,
        functools.partial(share_all, blocks=blocks),
        functools.partial(share, blocks=blocks),
        places,
        received,
    )
    return correlate(at, sources, received)


def solution(mesh):
    return jax.shard_map(
        shards,
        mesh=mesh,
        in_specs=(P(None, ("rblk", "chan"), None), P(), P()),
        out_specs=P("chan", None, None, "rblk"),
        check_vma=False,
    )
```

time: 92.4 us -> 76.9 us (0.83)
  Pallas kernels: 19.9 us -> 12.6 us
  blocking collectives: 24.1 us -> 19.4 us
  waiting for transfers between devices: 25.2 us -> 21.1 us
  other arithmetic: 0.54 us -> 3.2 us
  local copies, waits for them, and re-layouts: 2.75 us -> 0.09 us
    all_gather x1 -> x0, blocking collectives: 24.1 us -> none  [shards(): sources = lax.all_gather(picked, 'rblk', axis=0, tiled=False)]
    all_to_all x0 -> x1, blocking collectives: none -> 19.4 us  [share(): lax.all_to_all(flat, 'rblk', split_axis=0, concat_axis=0, tiled=True)]
    pallas_call x3 -> x2, Pallas kernels: 8.2 us -> 3.93 us  [the longest x1 3.28 us: correlate(): pl.pallas_call(correlate_kernel, out_shape=jax.ShapeDtypeStruct((NBIN, 2,...]
    all_to_all x1, waiting for transfers between devices: 25.2 us -> 21.1 us  [shards(): lax.all_to_all(flat, 'chan', split_axis=0, concat_axis=0, tiled=True)]
    pallas_call x1, Pallas kernels: 11.7 us -> 8.65 us  [spectra(): pl.pallas_call(spectra_kernel, out_shape=jax.ShapeDtypeStruct((NDEV * ROW...]
    unnamed x9 -> x4, local copies, waits for them, and re-layouts: 1.77 us -> 0.01 us
    reduce_sum x0 -> x3, other arithmetic: none -> 1.04 us  [the longest x1 0.72 us: plan(): total = jnp.sum(chosen, dtype=jnp.int32)]
    broadcast_in_dim x3 -> x0, local copies, waits for them, and re-layouts: 0.98 us -> none  [the longest x2 0.89 us: spectra(): band_edges[1:, None]]
  transfers between devices with their start and end apart: 1 -> 1, of which waited for: 1 -> 1; matrix products, arithmetic and copies ran while one was open for 1% -> 4% of each run, Pallas kernels for 0% -> 0%
where the time goes in v2:
time: 76.9 us; the launch traced here: 76.7 us
  waiting for transfers between devices  21.1 us (27%)
  starting transfers between devices  19.6 us (25%)
  blocking collectives  19.4 us (25%)
  Pallas kernels  12.6 us (16%)
  other arithmetic  3.2 us (4%)
    all_to_all x1, waiting for transfers between devices, shards(): lax.all_to_all(flat, 'chan', split_axis=0, concat_axis=0, tiled=True)  21.1 us
    all_to_all x1, starting transfers between devices, shards(): lax.all_to_all(flat, 'chan', split_axis=0, concat_axis=0, tiled=True)  19.6 us
    all_to_all x1, blocking collectives, share(): lax.all_to_all(flat, 'rblk', split_axis=0, concat_axis=0, tiled=True)  19.4 us
    pallas_call x1, Pallas kernels, spectra(): pl.pallas_call(spectra_kernel, out_shape=jax.ShapeDtypeStruct((NDEV * ROW...  8.65 us
    pallas_call x1, Pallas kernels, correlate(): pl.pallas_call(correlate_kernel, out_shape=jax.ShapeDtypeStruct((NBIN, 2,...  3.28 us
  transfers between devices with their start and end apart: 1, of which 1 were waited for; matrix products, arithmetic and copies ran while one was open for 4% of the time, Pallas kernels for 0%

profile of v2, /device:TPU:1, one launch (start us, length us, event | category | flops | bytes accessed | tf_op | source)
XLA Modules:
  0.0 76.7 jit_solution(3630479952365192330)
XLA Ops:
  0.0 0.0 copy-start
  0.0 0.0 copy-start.1
  0.0 8.6 %spectra.1 = f32[1920,128]{1,0:T(8,128)} custom-call(bf16[10,8,7680]{2,1,0:T(8,128)(2,1)} %bitcast.15, s32[33]{0:T(128)} %edge_hbm.1, f32[48,384]{1,0:T(8,128)} %constant.56.clone.tw_hbm, bf16[768,256]{1,0:T(8,128)(2,1)} %constant.57.clone.w_hbm), custom_call_target="tpu_custom_call" | custom-call | tf_op jit(solution)/shard_map/spectra/pallas_call | solution.py:255
  8.7 19.6 %all-to-all-start.1 = ((f32[64,1,3840]{2,1,0:T(1,128)}), f32[64,1,3840]{2,1,0:T(1,128)S(1)}, u32[]{:S(2)}, u32[]{:S(2)}) async-start(f32[64,1,3840]{2,1,0:T(1,128)} %bitcast.13), calls=%async_computation.1 | async-start | bytes 1966080 | tf_op jit(solution)/shard_map/all_to_all | solution.py:398
  28.3 0.0 copy-done.1
  28.3 0.7 convert_reduce_fusion.1
  29.0 0.2 convert_reduce_fusion
  29.2 0.7 compare_reduce_fusion
  30.5 0.1 pad.7.clone
  30.6 0.1 add_add_fusion
  30.7 0.1 select_reduce_fusion
  30.8 0.6 fusion.3.at_ref
  31.5 0.0 copy-done
  31.5 0.8 broadcast_select_fusion
  32.2 21.1 %all-to-all-done.1 = f32[64,1,3840]{2,1,0:T(1,128)S(1)} async-done(((f32[64,1,3840]{2,1,0:T(1,128)}), f32[64,1,3840]{2,1,0:T(1,128)S(1)}, u32[]{:S(2)}, u32[]{:S(2)}) %all-to-all-start.1) | async-done | bytes 983072 | tf_op jit(solution)/shard_map/all_to_all | solution.py:398
  53.3 20.1 %conditional.1 = (f32[480,128]{1,0:T(8,128)S(1)}) conditional(s32[]{:T(128)} %convert_element_type.12, (s32[3,64]{1,0:T(4,128)S(1)}, f32[1920,128]{1,0:T(8,128)S(1)}) %tuple.17, (s32[3,64]{1,0:T(4,128)S(1)}, f32[1920,128]{1,0:T(8,128)S(1)}) %tuple.18), branch_computations={%region_4.5_spmd, %region_5.7_spmd} | conditional | flops 172032 | bytes 2113552 | solution.py:399
  53.3 0.6 pick.2
  53.9 19.4 %all_to_all.9 = f32[8,1,7680]{2,1,0:T(1,128)S(1)} all-to-all(f32[8,1,7680]{2,1,0:T(1,128)S(1)} %bitcast.9), channel_id=1, replica_groups=mesh['chan'=64,'rblk'=8] {'rblk'}, dimensions={0} | all-to-all | bytes 491520 | tf_op jit(solution)/shard_map/cond/branch_0_fun/all_to_all | solution.py:384
  73.4 3.3 %correlate.1 = bf16[24,2,64,640]{3,2,1,0:T(8,128)(2,1)} custom-call(s32[64]{0:T(128)S(1)} %fusion.3.at_ref, f32[480,128]{1,0:T(8,128)S(1)} %get-tuple-element.24.src_ref, f32[1920,128]{1,0:T(8,128)S(1)} %bitcast.12), custom_call_target="tpu_custom_call" | custom-call | tf_op jit(solution)/shard_map/correlate/pallas_call | solution.py:346
  (2 shorter events, 0.0 us)
Async XLA Ops:
  0.0 31.5 %copy-start = (pred[3]{0:T(512)(128)(4,1)S(1)}, pred[3]{0:T(512)(128)(4,1)}, u32[]{:S(2)}) copy-start(pred[3]{0:T(512)(128)(4,1)} %constant.52.clone.1) | copy-start | bytes 13
  0.0 28.3 %copy-start.1 = (s32[64]{0:T(128)S(1)}, s32[64]{0:T(128)}, u32[]{:S(2)}) copy-start(s32[64]{0:T(128)} %param.8) | copy-start | bytes 772
  8.7 44.6 %all-to-all-start.1 = ((f32[64,1,3840]{2,1,0:T(1,128)}), f32[64,1,3840]{2,1,0:T(1,128)S(1)}, u32[]{:S(2)}, u32[]{:S(2)}) async-start(f32[64,1,3840]{2,1,0:T(1,128)} %bitcast.13), calls=%async_computation.1 | async-start | bytes 1966080 | tf_op jit(solution)/shard_map/all_to_all | solution.py:398

commit v3 on v2

--- a/solution.py
+++ b/solution.py
@@ -21,7 +21,7 @@
 HPAD = 384
 GROUPS = 3
 ROWS = GROUPS * CH
-ROOM = 20
+ROOM = 16
 RECV = NDEV * CH
 
 EPS = 1e-06
@@ -42,20 +42,18 @@
 @functools.lru_cache(maxsize=None)
 def tables():
     m = np.arange(HPAD)
-    inside = (m < HOP).astype(np.float64)
     s = np.arange(NBIN) + F_LOW
     angle = 2.0 * np.pi * ((s[:, None] * m[None, :]) % NSAMP) / NSAMP
-    twiddle = np.stack([np.cos(angle) * inside, -np.sin(angle) * inside], axis=1)
+    twiddle = np.stack([np.cos(angle), -np.sin(angle)], axis=1)
     d = np.arange(NDEV)
-    angle = 2.0 * np.pi * ((m[:, None] * d[None, :]) % HOP) / HOP
-    cos, sin = np.cos(angle) * inside[:, None], np.sin(angle) * inside[:, None]
-    w = np.stack([np.concatenate([cos, -sin], axis=1), np.concatenate([sin, cos], axis=1)])
-    w = w.reshape(2, 3, 128, 2 * NDEV).transpose(1, 0, 2, 3).reshape(2 * HPAD, 2 * NDEV)
-    w_hi, w_lo = split_np(w)
-    return (
-        twiddle.reshape(2 * NBIN, HPAD).astype(np.float32),
-        np.concatenate([w_hi, w_lo], axis=1),
-    )
+    angle = 2.0 * np.pi * ((m[:HOP, None] * d[None, :]) % HOP) / HOP
+    cos, sin = np.cos(angle), np.sin(angle)
+    of_re, of_im = np.concatenate([cos, -sin], axis=1), np.concatenate([sin, cos], axis=1)
+    cuts = [slice(0, 128), slice(128, 256), slice(256, HOP)]
+    w_hi, w_lo = split_np(np.concatenate([part[cut] for cut in cuts for part in (of_re, of_im)]))
+    both = np.concatenate([w_hi, w_lo], axis=1)
+    last = np.concatenate([w_hi[512:], np.zeros_like(w_lo[512:])], axis=1)
+    return twiddle.reshape(2 * NBIN, HPAD).astype(np.float32), np.concatenate([both, last])
 
 
 def split(x):
@@ -114,15 +112,16 @@
         return pltpu.make_async_copy(rec_hbm.at[i], rec_ref.at[i], rec_sems.at[i])
 
     small = [(edge_hbm, edge_ref), (tw_hbm, tw_ref), (w_hbm, w_ref)]
-    copies = [pltpu.make_async_copy(a, b, sems.at[k]) for k, (a, b) in enumerate(small)]
-    copies[0].start()
+    edge_copy, tw_copy, w_copy = [pltpu.make_async_copy(a, b, sems.at[k]) for k, (a, b) in enumerate(small)]
+    edge_copy.start()
     fetch(0).start()
-    copies[1].start()
-    copies[2].start()
-    for i in range(1, CH):
+    tw_copy.start()
+    fetch(1).start()
+    w_copy.start()
+    for i in range(2, CH):
         fetch(i).start()
 
-    copies[0].wait()
+    edge_copy.wait()
     shape = (NB, 128)
     row = lax.broadcasted_iota(jnp.int32, shape, 0)
     low, high = jnp.zeros(shape, jnp.int32), jnp.zeros(shape, jnp.int32)
@@ -136,8 +135,7 @@
     for s in range(NBIN):
         inside = (start + s >= low) & (start + s < high)
         m_ref[:, pl.ds(s * 128, 128)] = jnp.where(inside, 1.0, 0.0).astype(BF16)
-    copies[1].wait()
-    copies[2].wait()
+    tw_copy.wait()
 
     lane = lax.broadcasted_iota(jnp.int32, (SEG, 128), 1)
     low_half = lane < 64
@@ -179,67 +177,71 @@
                     else:
                         res.append(re * c - im * e)
                         ims.append(re * e + im * c)
+                rows = pl.ds(pair * 16, 16)
+                if q == 2:
+                    values = [jnp.where(low_half, r, pltpu.roll(i, 64, 1)) for r, i in zip(res, ims)]
+                    hi, lo = split(jnp.concatenate(values, axis=0))
+                    a_ref[4, rows, pl.ds(0, 128)] = hi
+                    a_ref[4, rows, pl.ds(128, 128)] = lo
+                    continue
                 for part, values in enumerate((res, ims)):
                     hi, lo = split(jnp.concatenate(values, axis=0))
-                    a_ref[q, 0, pl.ds(pair * 16, 16), pl.ds(part * 128, 128)] = hi
-                    a_ref[q, 1, pl.ds(pair * 16, 16), pl.ds(part * 128, 128)] = lo
-
-    def multiply(place, a_ref):
-        z = None
-        for q in range(3):
-            depth = pl.ds(q * 256, 256)
-            both = jnp.dot(a_ref[q, 0], w_ref[depth, :], preferred_element_type=F32)
-            rest = jnp.dot(a_ref[q, 1], w_ref[depth, pl.ds(0, 128)], preferred_element_type=F32)
-            term = (both[:, :128] + both[:, 128:]) + rest
-            z = term if z is None else z + term
-        z_ref[pl.ds(pl.multiple_of(place * NBIN * SEG, NBIN * SEG), NBIN * SEG), :] = z
+                    a_ref[q, rows, pl.ds(part * 128, 128)] = hi
+                    a_ref[2 + q, rows, pl.ds(part * 128, 128)] = lo
+
+    def multiply(i, a_ref):
+        both = jnp.dot(a_ref[0], w_ref[pl.ds(0, 256), :], preferred_element_type=F32)
+        both = both + jnp.dot(a_ref[1], w_ref[pl.ds(256, 256), :], preferred_element_type=F32)
+        both = both + jnp.dot(a_ref[4], w_ref[pl.ds(512, 256), :], preferred_element_type=F32)
+        rest = jnp.dot(a_ref[2], w_ref[pl.ds(0, 256), pl.ds(0, 128)], preferred_element_type=F32)
+        rest = rest + jnp.dot(a_ref[3], w_ref[pl.ds(256, 256), pl.ds(0, 128)], preferred_element_type=F32)
+        z = (both[:, :128] + both[:, 128:]) + rest
+        z_ref[pl.ds(i * NBIN * SEG, NBIN * SEG), :] = z
         for s in range(NBIN):
             v = z[s * SEG : (s + 1) * SEG]
-            p_ref[pl.ds(pl.multiple_of(place * SEG, SEG), SEG), pl.ds(s * 128, 128)] = v * v
-
-    def two_channels(j, carry):
-        fetch(2 * j).wait()
-        fetch(2 * j + 1).wait()
-        multiply(2 * j, odd_ref)
-        transform(2 * j, even_ref)
-        multiply(2 * j + 1, even_ref)
-        transform(2 * j + 1, odd_ref)
-        return carry
-
-    lax.fori_loop(0, CH // 2, two_channels, 0)
-    multiply(CH, odd_ref)
-
-    member = m_ref[...]
-    rows = CH * SEG
-    power = jnp.concatenate(split(p_ref[pl.ds(SEG, rows), :]), axis=0)
-    band = lax.dot_general(power, member, NT, preferred_element_type=F32)
-    band = band[:rows] + band[rows:]
-    scale = lax.rsqrt(band / widths + EPS)
-    s_hi = scale.astype(BF16)
-    rest = scale - s_hi.astype(F32)
-    s_mid, s_lo = split(rest)
-    scales = jnp.concatenate([s_hi, s_mid, s_lo], axis=1)
-    copied = jnp.concatenate([member] * 3, axis=0)
-    per_bin = jnp.dot(scales, copied, preferred_element_type=F32)
-    p_ref[pl.ds(SEG, CH * SEG), :] = per_bin
+            p_ref[pl.ds(i * SEG, SEG), pl.ds(s * 128, 128)] = v * v
 
     half64 = lax.broadcasted_iota(jnp.int32, (64, 128), 1) < 64
-    where = [(t, i) for i in range(CH) for t in range(GROUPS)]
+
+    def whiten():
+        rows = CH * SEG
+        member = m_ref[...]
+        power = jnp.concatenate(split(p_ref[...]), axis=0)
+        band = lax.dot_general(power, member, NT, preferred_element_type=F32)
+        scale = lax.rsqrt((band[:rows] + band[rows:]) / widths + EPS)
+        s_hi = scale.astype(BF16)
+        s_mid, s_lo = split(scale - s_hi.astype(F32))
+        scales = jnp.concatenate([s_hi, s_mid, s_lo], axis=1)
+        copied = jnp.concatenate([member] * 3, axis=0)
+        p_ref[...] = jnp.dot(scales, copied, preferred_element_type=F32)
 
     def whitened(t, i):
-        z = z_ref[pl.ds((i + 1) * NBIN * SEG + t * 64, 64), :]
-        factor = [p_ref[pl.ds((i + 1) * SEG, SEG), pl.ds((t * 8 + u) * 128, 128)] for u in range(8)]
+        z = z_ref[pl.ds(i * NBIN * SEG + t * 64, 64), :]
+        factor = [p_ref[pl.ds(i * SEG, SEG), pl.ds((t * 8 + u) * 128, 128)] for u in range(8)]
         return z * jnp.concatenate(factor, axis=0)
 
-    for k in range(0, len(where), 2):
-        first, second = whitened(*where[k]), whitened(*where[k + 1])
+    def place(*pair):
+        first, second = (whitened(t, i) for t, i in pair)
         upper = jnp.where(half64, first, pltpu.roll(second, 64, 1))
         lower = jnp.where(half64, pltpu.roll(first, 64, 1), second)
         halves = [h[u * SEG : (u + 1) * SEG] for u in range(8) for h in (upper, lower)]
         turned = jnp.concatenate(halves, axis=0).T
-        for part in range(2):
-            t, i = where[k + part]
+        for part, (t, i) in enumerate(pair):
             out_ref[pl.ds(t * CH + i, NDEV, stride=ROWS), :] = turned[part * 64 : part * 64 + 64]
+
+    a_refs = (even_ref, odd_ref)
+    for i in range(CH):
+        fetch(i).wait()
+        if i:
+            multiply(i - 1, a_refs[(i - 1) % 2])
+        transform(i, a_refs[i % 2])
+        if i == 0:
+            w_copy.wait()
+    multiply(CH - 1, a_refs[(CH - 1) % 2])
+    whiten()
+    for i in range(0, CH, 2):
+        for t in range(GROUPS):
+            place((t, i), (t, i + 1))
 
 
 def vmem():
@@ -259,10 +261,10 @@
         out_specs=vmem(),
         scratch_shapes=[
             pltpu.VMEM((CH, SEG, NSAMP), BF16),
-            pltpu.VMEM((3, 2, NBIN * SEG, 256), BF16),
-            pltpu.VMEM((3, 2, NBIN * SEG, 256), BF16),
-            pltpu.VMEM(((CH + 1) * NBIN * SEG, 128), F32),
-            pltpu.VMEM(((CH + 1) * SEG, NBIN * 128), F32),
+            pltpu.VMEM((5, NBIN * SEG, 256), BF16),
+            pltpu.VMEM((5, NBIN * SEG, 256), BF16),
+            pltpu.VMEM((CH * NBIN * SEG, 128), F32),
+            pltpu.VMEM((CH * SEG, NBIN * 128), F32),
             pltpu.VMEM((NB, NBIN * 128), BF16),
             pltpu.VMEM(twiddle.shape, F32),
             pltpu.VMEM(w.shape, BF16),
@@ -301,9 +303,11 @@
     )(places, received)
 
 
-def correlate_kernel(at_ref, src_ref, recv_ref, out_hbm, left_ref, right_ref, dense_ref, s_ref, out_ref, sems):
-    for k in range(NS):
-        s_ref[pl.ds(k * GROUPS, GROUPS), :] = src_ref[pl.ds(at_ref[k], GROUPS), :]
+def correlate_kernel(
+    at_hbm, src_ref, recv_ref, out_hbm, left_ref, right_ref, dense_ref, s_ref, out_ref, at_ref, at_sem, sems
+):
+    table = pltpu.make_async_copy(at_hbm, at_ref, at_sem)
+    table.start()
     lower = lax.broadcasted_iota(jnp.int32, (RECV, 128), 1) < 64
     lane = lax.broadcasted_iota(jnp.int32, (2 * NS, 128), 1)
     imag = lane[:NS] & SEG != 0
@@ -319,6 +323,10 @@
         right_ref[t, 1] = jnp.where(lower, turned, hi)
         right_ref[t, 2] = hi
 
+        if t == 0:
+            table.wait()
+            for k in range(NS):
+                s_ref[pl.ds(k * GROUPS, GROUPS), :] = src_ref[pl.ds(at_ref[k], GROUPS), :]
         s = s_ref[pl.ds(t, NS, stride=GROUPS), :] * (1.0 / SEG)
         crossed = jnp.where(imag, pltpu.roll(s, SEG, 1), -pltpu.roll(s, 128 - SEG, 1))
         hi, lo = split(jnp.concatenate([s, crossed], axis=0))
@@ -332,11 +340,14 @@
                 left_ref[part, rows, pl.ds(0, 128)] = jnp.where(which % 4 == v, both, 0.0).astype(BF16)
                 left_ref[part, rows, pl.ds(128, 128)] = jnp.where(which == 4 * h + v, lo, 0.0).astype(BF16)
             right = jnp.concatenate([right_ref[t, h], right_ref[t, 2]], axis=1)
-            result = lax.dot_general(left_ref[part], right, NT, preferred_element_type=F32)
-            bins = pl.ds(4 * part, 4)
-            out_ref[bins] = result.astype(BF16).reshape(4, 2, NS, RECV)
-            copies.append(pltpu.make_async_copy(out_ref.at[bins], out_hbm.at[bins], sems.at[part]))
-            copies[-1].start()
+            for w in range(2):
+                left = left_ref[part, pl.ds(w * 4 * NS, 4 * NS)]
+                result = lax.dot_general(left, right, NT, preferred_element_type=F32)
+                piece = 2 * part + w
+                bins = pl.ds(2 * piece, 2)
+                out_ref[bins] = result.astype(BF16).reshape(2, 2, NS, RECV)
+                copies.append(pltpu.make_async_copy(out_ref.at[bins], out_hbm.at[bins], sems.at[piece]))
+                copies[-1].start()
     for copy in copies:
         copy.wait()
 
@@ -346,7 +357,7 @@
     return pl.pallas_call(
         correlate_kernel,
         out_shape=jax.ShapeDtypeStruct((NBIN, 2, NS, RECV), BF16),
-        in_specs=[smem(), vmem(), vmem()],
+        in_specs=[pl.BlockSpec(memory_space=pltpu.HBM), vmem(), vmem()],
         out_specs=pl.BlockSpec(memory_space=pltpu.HBM),
         scratch_shapes=[
             pltpu.VMEM((parts, 8 * NS, 256), BF16),
@@ -354,7 +365,9 @@
             pltpu.VMEM((GROUPS, RECV, 128), F32),
             pltpu.VMEM((NS * GROUPS, 128), F32),
             pltpu.VMEM((NBIN, 2, NS, RECV), BF16),
-            pltpu.SemaphoreType.DMA((parts,)),
+            pltpu.SMEM((NS,), jnp.int32),
+            pltpu.SemaphoreType.DMA,
+            pltpu.SemaphoreType.DMA((2 * parts,)),
         ],
         compiler_params=pltpu.CompilerParams(vmem_limit_bytes=VMEM_LIMIT),
         name="correlate",

time: 76.9 us -> 74 us (0.962)
  blocking collectives: 19.4 us -> 17.3 us
  Pallas kernels: 12.6 us -> 11.6 us
    all_to_all x1, blocking collectives: 19.4 us -> 17.3 us  [share(): lax.all_to_all(flat, 'rblk', split_axis=0, concat_axis=0, tiled=True)]
where the time goes in v3:
time: 74 us; the launch traced here: 73.7 us
  waiting for transfers between devices  21.2 us (29%)
  starting transfers between devices  19.6 us (26%)
  blocking collectives  17.3 us (23%)
  Pallas kernels  11.6 us (16%)
  other arithmetic  3.2 us (4%)
    all_to_all x1, waiting for transfers between devices, shards(): lax.all_to_all(flat, 'chan', split_axis=0, concat_axis=0, tiled=True)  21.2 us
    all_to_all x1, starting transfers between devices, shards(): lax.all_to_all(flat, 'chan', split_axis=0, concat_axis=0, tiled=True)  19.6 us
    all_to_all x1, blocking collectives, share(): lax.all_to_all(flat, 'rblk', split_axis=0, concat_axis=0, tiled=True)  17.3 us
    pallas_call x1, Pallas kernels, spectra(): pl.pallas_call(spectra_kernel, out_shape=jax.ShapeDtypeStruct((NDEV * ROW...  7.92 us
    pallas_call x1, Pallas kernels, correlate(): pl.pallas_call(correlate_kernel, out_shape=jax.ShapeDtypeStruct((NBIN, 2,...  3.08 us
  transfers between devices with their start and end apart: 1, of which 1 were waited for; matrix products, arithmetic and copies ran while one was open for 4% of the time, Pallas kernels for 0%

profile of v3, /device:TPU:1, one launch (start us, length us, event | category | flops | bytes accessed | tf_op | source)
XLA Modules:
  0.0 73.7 jit_solution(9284429689255496505)
XLA Ops:
  0.0 0.0 copy-start
  0.0 0.0 copy-start.1
  0.0 7.9 %spectra.1 = f32[1920,128]{1,0:T(8,128)} custom-call(bf16[10,8,7680]{2,1,0:T(8,128)(2,1)} %bitcast.15, s32[33]{0:T(128)} %edge_hbm.1, f32[48,384]{1,0:T(8,128)} %constant.56.clone.tw_hbm, bf16[768,256]{1,0:T(8,128)(2,1)} %constant.57.clone.w_hbm), custom_call_target="tpu_custom_call" | custom-call | tf_op jit(solution)/shard_map/spectra/pallas_call | solution.py:257
  7.9 19.6 %all-to-all-start.1 = ((f32[64,1,3840]{2,1,0:T(1,128)}), f32[64,1,3840]{2,1,0:T(1,128)S(1)}, u32[]{:S(2)}, u32[]{:S(2)}) async-start(f32[64,1,3840]{2,1,0:T(1,128)} %bitcast.13), calls=%async_computation.1 | async-start | bytes 1966080 | tf_op jit(solution)/shard_map/all_to_all | solution.py:411
  27.6 0.0 copy-done.1
  27.6 0.7 convert_reduce_fusion.1
  28.3 0.2 convert_reduce_fusion
  28.5 0.7 compare_reduce_fusion
  29.8 0.1 pad.7.clone
  29.9 0.1 add_add_fusion
  29.9 0.1 select_reduce_fusion
  30.1 0.6 fusion.3.at_hbm
  30.7 0.0 copy-done
  30.7 0.8 %broadcast_select_fusion = s32[3,64]{1,0:T(4,128)S(1)} fusion(s32[3,64]{1,0:T(4,128)S(1)} %select_reduce_fusion, s32[]{:T(128)} %get-tuple-element.20, pred[3]{0:T(512)(128)(4,1)S(1)} %copy-done), kind=kLoop, calls=%fused_computation.12 | loop fusion | flops 192 | bytes 1543 | tf_op jit(solution)/shard_map/concatenate | solution.py:389
  31.5 21.2 %all-to-all-done.1 = f32[64,1,3840]{2,1,0:T(1,128)S(1)} async-done(((f32[64,1,3840]{2,1,0:T(1,128)}), f32[64,1,3840]{2,1,0:T(1,128)S(1)}, u32[]{:S(2)}, u32[]{:S(2)}) %all-to-all-start.1) | async-done | bytes 983072 | tf_op jit(solution)/shard_map/all_to_all | solution.py:411
  52.7 18.0 %conditional.1 = (f32[384,128]{1,0:T(8,128)S(1)}) conditional(s32[]{:T(128)} %convert_element_type.12, (s32[3,64]{1,0:T(4,128)S(1)}, f32[1920,128]{1,0:T(8,128)S(1)}) %tuple.17, (s32[3,64]{1,0:T(4,128)S(1)}, f32[1920,128]{1,0:T(8,128)S(1)}) %tuple.18), branch_computations={%region_4.5_spmd, %region_5.7_spmd} | conditional | flops 172032 | bytes 2064400 | solution.py:412
  52.7 0.7 pick.2
  53.4 17.3 %all_to_all.9 = f32[8,1,6144]{2,1,0:T(1,128)S(1)} all-to-all(f32[8,1,6144]{2,1,0:T(1,128)S(1)} %bitcast.9), channel_id=1, replica_groups=mesh['chan'=64,'rblk'=8] {'rblk'}, dimensions={0} | all-to-all | bytes 393216 | tf_op jit(solution)/shard_map/cond/branch_0_fun/all_to_all | solution.py:397
  70.7 3.1 %correlate.1 = bf16[24,2,64,640]{3,2,1,0:T(8,128)(2,1)} custom-call(s32[64]{0:T(128)S(1)} %fusion.3.at_hbm, f32[384,128]{1,0:T(8,128)S(1)} %get-tuple-element.24.src_ref, f32[1920,128]{1,0:T(8,128)S(1)} %bitcast.12), custom_call_target="tpu_custom_call" | custom-call | tf_op jit(solution)/shard_map/correlate/pallas_call | solution.py:357
  (2 shorter events, 0.0 us)
Async XLA Ops:
  0.0 30.7 %copy-start = (pred[3]{0:T(512)(128)(4,1)S(1)}, pred[3]{0:T(512)(128)(4,1)}, u32[]{:S(2)}) copy-start(pred[3]{0:T(512)(128)(4,1)} %constant.52.clone.1) | copy-start | bytes 13
  0.0 27.6 %copy-start.1 = (s32[64]{0:T(128)S(1)}, s32[64]{0:T(128)}, u32[]{:S(2)}) copy-start(s32[64]{0:T(128)} %param.8) | copy-start | bytes 772
  7.9 44.8 %all-to-all-start.1 = ((f32[64,1,3840]{2,1,0:T(1,128)}), f32[64,1,3840]{2,1,0:T(1,128)S(1)}, u32[]{:S(2)}, u32[]{:S(2)}) async-start(f32[64,1,3840]{2,1,0:T(1,128)} %bitcast.13), calls=%async_computation.1 | async-start | bytes 1966080 | tf_op jit(solution)/shard_map/all_to_all | solution.py:411

commit v4 on v3

--- a/solution.py
+++ b/solution.py
@@ -303,15 +303,21 @@
     )(places, received)
 
 
-def correlate_kernel(
-    at_hbm, src_ref, recv_ref, out_hbm, left_ref, right_ref, dense_ref, s_ref, out_ref, at_ref, at_sem, sems
-):
-    table = pltpu.make_async_copy(at_hbm, at_ref, at_sem)
-    table.start()
+def correlate_kernel(chosen_ref, src_ref, recv_ref, out_hbm, left_ref, right_ref, dense_ref, out_ref, sems):
+    places = chosen_ref.shape[1]
     lower = lax.broadcasted_iota(jnp.int32, (RECV, 128), 1) < 64
     lane = lax.broadcasted_iota(jnp.int32, (2 * NS, 128), 1)
     imag = lane[:NS] & SEG != 0
     which = lane // (2 * SEG)
+    sources = []
+    for t in range(GROUPS):
+        parts = jnp.concatenate(split(src_ref[pl.ds(t, places, stride=GROUPS), :] * (1.0 / SEG)), axis=1)
+        s = jnp.dot(chosen_ref[...], parts, preferred_element_type=F32)
+        hi, lo = (
+            jnp.concatenate([v, jnp.where(imag, pltpu.roll(v, SEG, 1), -pltpu.roll(v, 128 - SEG, 1))], axis=0)
+            for v in (s[:, :128], s[:, 128:])
+        )
+        sources.append((hi, lo))
     copies = []
     for t in range(GROUPS):
         for i in range(CH):
@@ -323,14 +329,7 @@
         right_ref[t, 1] = jnp.where(lower, turned, hi)
         right_ref[t, 2] = hi
 
-        if t == 0:
-            table.wait()
-            for k in range(NS):
-                s_ref[pl.ds(k * GROUPS, GROUPS), :] = src_ref[pl.ds(at_ref[k], GROUPS), :]
-        s = s_ref[pl.ds(t, NS, stride=GROUPS), :] * (1.0 / SEG)
-        crossed = jnp.where(imag, pltpu.roll(s, SEG, 1), -pltpu.roll(s, 128 - SEG, 1))
-        hi, lo = split(jnp.concatenate([s, crossed], axis=0))
-        hi, lo = hi.astype(F32), lo.astype(F32)
+        hi, lo = sources[t]
         hi_turned = pltpu.roll(hi, 64, 1)
         for h in range(2):
             part = 2 * t + h
@@ -352,29 +351,26 @@
         copy.wait()
 
 
-def correlate(at, sources, received):
+def correlate(chosen, sources, received):
     parts = 2 * GROUPS
     return pl.pallas_call(
         correlate_kernel,
         out_shape=jax.ShapeDtypeStruct((NBIN, 2, NS, RECV), BF16),
-        in_specs=[pl.BlockSpec(memory_space=pltpu.HBM), vmem(), vmem()],
+        in_specs=[vmem()] * 3,
         out_specs=pl.BlockSpec(memory_space=pltpu.HBM),
         scratch_shapes=[
             pltpu.VMEM((parts, 8 * NS, 256), BF16),
             pltpu.VMEM((GROUPS, 3, RECV, 128), BF16),
             pltpu.VMEM((GROUPS, RECV, 128), F32),
-            pltpu.VMEM((NS * GROUPS, 128), F32),
             pltpu.VMEM((NBIN, 2, NS, RECV), BF16),
-            pltpu.SMEM((NS,), jnp.int32),
-            pltpu.SemaphoreType.DMA,
             pltpu.SemaphoreType.DMA((2 * parts,)),
         ],
         compiler_params=pltpu.CompilerParams(vmem_limit_bytes=VMEM_LIMIT),
         name="correlate",
-    )(at, sources, received)
-
-
-def plan(source_index, block):
+    )(chosen, sources, received)
+
+
+def plan(source_index, block, blocks):
     owner, local = source_index // RECV, source_index % RECV
     number = jnp.arange(NS, dtype=jnp.int32)
     same = owner[:, None] == owner[None, :]
@@ -387,8 +383,9 @@
     places = jnp.sum(jnp.where(to, columns, 0), axis=2)
     total = jnp.sum(chosen, dtype=jnp.int32)
     places = jnp.concatenate([places[:2], jnp.broadcast_to(total, (1, NS))])
-    at = GROUPS * jnp.where(crowded, number, owner * ROOM + rank)
-    return places, at, crowded
+    at = jnp.where(crowded, number, owner * ROOM + rank)
+    moved = at[:, None] == jnp.arange(blocks * ROOM, dtype=jnp.int32)[None, :]
+    return places, moved.astype(F32).astype(BF16), crowded
 
 
 def share(places, received, blocks):
@@ -405,7 +402,7 @@
 
 def shards(records, source_index, band_edges):
     blocks = lax.axis_size("rblk")
-    places, at, crowded = plan(source_index, lax.axis_index("rblk"))
+    places, chosen, crowded = plan(source_index, lax.axis_index("rblk"), blocks)
     sent = spectra(jnp.transpose(records, (1, 0, 2)), band_edges)
     flat = sent.reshape(NDEV, 1, ROWS * 128)
     received = lax.all_to_all(flat, "chan", split_axis=0, concat_axis=0, tiled=True).reshape(sent.shape)
@@ -416,7 +413,7 @@
         places,
         received,
     )
-    return correlate(at, sources, received)
+    return correlate(chosen, sources, received)
 
 
 def solution(mesh):

time: 74 us -> 73.7 us (level)
  transfers between devices with their start and end apart: 1 -> 1, of which waited for: 1 -> 1; matrix products, arithmetic and copies ran while one was open for 4% -> 5% of each run, Pallas kernels for 0% -> 0%
where the time goes in v4:
time: 73.7 us; the launch traced here: 73.4 us
  waiting for transfers between devices  21.1 us (29%)
  starting transfers between devices  19.6 us (27%)
  blocking collectives  17.3 us (23%)
  Pallas kernels  11.3 us (15%)
  other arithmetic  3.27 us (4%)
    all_to_all x1, waiting for transfers between devices, shards(): lax.all_to_all(flat, 'chan', split_axis=0, concat_axis=0, tiled=True)  21.1 us
    all_to_all x1, starting transfers between devices, shards(): lax.all_to_all(flat, 'chan', split_axis=0, concat_axis=0, tiled=True)  19.6 us
    all_to_all x1, blocking collectives, share(): lax.all_to_all(flat, 'rblk', split_axis=0, concat_axis=0, tiled=True)  17.3 us
    pallas_call x1, Pallas kernels, spectra(): pl.pallas_call(spectra_kernel, out_shape=jax.ShapeDtypeStruct((NDEV * ROW...  7.92 us
    pallas_call x1, Pallas kernels, correlate(): pl.pallas_call(correlate_kernel, out_shape=jax.ShapeDtypeStruct((NBIN, 2,...  2.73 us
  transfers between devices with their start and end apart: 1, of which 1 were waited for; matrix products, arithmetic and copies ran while one was open for 5% of the time, Pallas kernels for 0%

profile of v4, /device:TPU:1, one launch (start us, length us, event | category | flops | bytes accessed | tf_op | source)
XLA Modules:
  0.0 73.4 jit_solution(3844897228512056031)
XLA Ops:
  0.0 0.0 copy-start
  0.0 0.0 copy-start.1
  0.0 7.9 %spectra.1 = f32[1920,128]{1,0:T(8,128)} custom-call(bf16[10,8,7680]{2,1,0:T(8,128)(2,1)} %bitcast.15, s32[33]{0:T(128)} %edge_hbm.1, f32[48,384]{1,0:T(8,128)} %constant.54.clone.tw_hbm, bf16[768,256]{1,0:T(8,128)(2,1)} %constant.55.clone.w_hbm), custom_call_target="tpu_custom_call" | custom-call | tf_op jit(solution)/shard_map/spectra/pallas_call | solution.py:257
  7.9 19.6 %all-to-all-start.1 = ((f32[64,1,3840]{2,1,0:T(1,128)}), f32[64,1,3840]{2,1,0:T(1,128)S(1)}, u32[]{:S(2)}, u32[]{:S(2)}) async-start(f32[64,1,3840]{2,1,0:T(1,128)} %bitcast.13), calls=%async_computation.1 | async-start | bytes 1966080 | tf_op jit(solution)/shard_map/all_to_all | solution.py:408
  27.6 0.0 copy-done.1
  27.6 0.7 convert_reduce_fusion.1
  28.3 0.2 convert_reduce_fusion
  28.5 0.7 compare_reduce_fusion
  29.8 0.1 pad.7.clone
  29.9 0.1 add_add_fusion
  29.9 0.1 select_reduce_fusion
  30.1 0.6 broadcast_select_fusion.1
  30.7 0.0 copy-done
  30.7 0.8 %broadcast_select_fusion = s32[3,64]{1,0:T(4,128)S(1)} fusion(s32[3,64]{1,0:T(4,128)S(1)} %select_reduce_fusion, s32[]{:T(128)} %get-tuple-element.20, pred[3]{0:T(512)(128)(4,1)S(1)} %copy-done), kind=kLoop, calls=%fused_computation.14 | loop fusion | flops 192 | bytes 1543 | tf_op jit(solution)/shard_map/concatenate | solution.py:385
  31.5 0.1 convert_convert_fusion.chosen_ref
  31.6 21.1 %all-to-all-done.1 = f32[64,1,3840]{2,1,0:T(1,128)S(1)} async-done(((f32[64,1,3840]{2,1,0:T(1,128)}), f32[64,1,3840]{2,1,0:T(1,128)S(1)}, u32[]{:S(2)}, u32[]{:S(2)}) %all-to-all-start.1) | async-done | bytes 983072 | tf_op jit(solution)/shard_map/all_to_all | solution.py:408
  52.7 18.0 %conditional.1 = (f32[384,128]{1,0:T(8,128)S(1)}) conditional(s32[]{:T(128)} %convert_element_type.20, (s32[3,64]{1,0:T(4,128)S(1)}, f32[1920,128]{1,0:T(8,128)S(1)}) %tuple.17, (s32[3,64]{1,0:T(4,128)S(1)}, f32[1920,128]{1,0:T(8,128)S(1)}) %tuple.18), branch_computations={%region_4.5_spmd, %region_5.7_spmd} | conditional | flops 172032 | bytes 2064400 | solution.py:409
  52.7 0.6 pick.2
  53.3 17.3 %all_to_all.9 = f32[8,1,6144]{2,1,0:T(1,128)S(1)} all-to-all(f32[8,1,6144]{2,1,0:T(1,128)S(1)} %bitcast.9), channel_id=1, replica_groups=mesh['chan'=64,'rblk'=8] {'rblk'}, dimensions={0} | all-to-all | bytes 393216 | tf_op jit(solution)/shard_map/cond/branch_0_fun/all_to_all | solution.py:394
  70.7 2.7 %correlate.1 = bf16[24,2,64,640]{3,2,1,0:T(8,128)(2,1)} custom-call(bf16[64,128]{1,0:T(8,128)(2,1)S(1)} %convert_convert_fusion.chosen_ref, f32[384,128]{1,0:T(8,128)S(1)} %get-tuple-element.24.src_ref, f32[1920,128]{1,0:T(8,128)S(1)} %bitcast.12), custom_call_target="tpu_custom_call" | custom-call | tf_op jit(solution)/shard_map/correlate/pallas_call | solution.py:356
  (2 shorter events, 0.0 us)
Async XLA Ops:
  0.0 30.7 %copy-start = (pred[3]{0:T(512)(128)(4,1)S(1)}, pred[3]{0:T(512)(128)(4,1)}, u32[]{:S(2)}) copy-start(pred[3]{0:T(512)(128)(4,1)} %constant.50.clone.1) | copy-start | bytes 13
  0.0 27.6 %copy-start.1 = (s32[64]{0:T(128)S(1)}, s32[64]{0:T(128)}, u32[]{:S(2)}) copy-start(s32[64]{0:T(128)} %param.8) | copy-start | bytes 772
  7.9 44.8 %all-to-all-start.1 = ((f32[64,1,3840]{2,1,0:T(1,128)}), f32[64,1,3840]{2,1,0:T(1,128)S(1)}, u32[]{:S(2)}, u32[]{:S(2)}) async-start(f32[64,1,3840]{2,1,0:T(1,128)} %bitcast.13), calls=%async_computation.1 | async-start | bytes 1966080 | tf_op jit(solution)/shard_map/all_to_all | solution.py:408
